TPU v7x, 32 devices: a whole 2x2x4 slice. The times are simulated.
32 devices in a mesh: dp: 2 (over core), row: 4 (over y, x), col: 4 (over z).
Axes of the slice: x: 2, y: 2, z: 4, core: 2. Of those that a mesh axis runs over, the one named last changes fastest.
Arguments:
- inputs: bfloat16 [8192, 512], P('dp', ('row', 'col')), may hold values from -6 to 6
- memory: bfloat16 [2048, 512], P('dp', ('row', 'col')), may hold values from -6 to 6
- teacher: bfloat16 [8192, 512], P('dp', ('row', 'col')), may hold values from -6 to 6
- segment_ids: int32 [8192], P('dp'), may hold values from 0 to 12, as said below
- parent_ids: int32 [8192], P('dp'), may hold values from -1 to 10, as said below
- valid_length: int32 [2], P('dp'), may hold values from 1024 to 4096
- query_weight: bfloat16 [512, 512], P('row', 'col'), may hold values from -0.25 to 0.25
- query_bias: bfloat16 [512], P('col'), may hold values from -3 to 3
- key_weight: bfloat16 [512, 512], P('row', 'col'), may hold values from -0.25 to 0.25
- value_weight: bfloat16 [512, 512], P('row', 'col'), may hold values from -0.25 to 0.25
- value_bias: bfloat16 [512], P('col'), may hold values from -3 to 3
- proj_weight: bfloat16 [512, 512], P('col', 'row'), may hold values from -1 to 1
- proj_bias: bfloat16 [512], P('row'), may hold values from -3 to 3
- cross_query_weight: bfloat16 [512, 512], P('row', 'col'), may hold values from -0.25 to 0.25
- cross_query_bias: bfloat16 [512], P('col'), may hold values from -3 to 3
- cross_key_weight: bfloat16 [512, 512], P('row', 'col'), may hold values from -0.25 to 0.25
- cross_value_weight: bfloat16 [512, 512], P('row', 'col'), may hold values from -0.25 to 0.25
- cross_value_bias: bfloat16 [512], P('col'), may hold values from -3 to 3
- cross_proj_weight: bfloat16 [512, 512], P('col', 'row'), may hold values from -1 to 1
- cross_proj_bias: bfloat16 [512], P('row'), may hold values from -3 to 3
- up_weight: bfloat16 [512, 2048], P('row', 'col'), may hold values from -0.25 to 0.25
- up_bias: bfloat16 [2048], P('col'), may hold values from -3 to 3
- down_weight: bfloat16 [2048, 512], P('col', 'row'), may hold values from -0.125 to 0.125
- down_bias: bfloat16 [512], P('row'), may hold values from -3 to 3
Outputs:
- output: bfloat16 [8192, 512], P('dp', ('row', 'col'))
- mean_loss: float32 [], replicated
- grad_input: float32 [8192, 512], P('dp', ('row', 'col'))
- grad_memory: float32 [2048, 512], P('dp', ('row', 'col'))
- grad_query_weight: float32 [512, 512], P('row', 'col')
- grad_query_bias: float32 [512], P('col')
- grad_key_weight: float32 [512, 512], P('row', 'col')
- grad_value_weight: float32 [512, 512], P('row', 'col')
- grad_value_bias: float32 [512], P('col')
- grad_proj_weight: float32 [512, 512], P('col', 'row')
- grad_proj_bias: float32 [512], P('row')
- grad_cross_query_weight: float32 [512, 512], P('row', 'col')
- grad_cross_query_bias: float32 [512], P('col')
- grad_cross_key_weight: float32 [512, 512], P('row', 'col')
- grad_cross_value_weight: float32 [512, 512], P('row', 'col')
- grad_cross_value_bias: float32 [512], P('col')
- grad_cross_proj_weight: float32 [512, 512], P('col', 'row')
- grad_cross_proj_bias: float32 [512], P('row')
- grad_up_weight: float32 [512, 2048], P('row', 'col')
- grad_up_bias: float32 [2048], P('col')
- grad_down_weight: float32 [2048, 512], P('col', 'row')
- grad_down_bias: float32 [512], P('row')
Inputs may be any that keep to these rules, and one draw needn't show every extreme that they name: `segment_ids`: within each tree of 4096 positions the segment ids never fall; 0 is the trunk, then four groups follow, each a branch and its two leaves (ids 1 to 12 in that order); every segment has one position or more. `parent_ids`: the parent segment of the token's segment: -1 in the trunk, 0 in a branch, the branch's id in a leaf.
All inputs are finite; a program needn't handle non-finite values.
Results may differ from a plain program's by a relative error of at most 0.03.
The roundings to bfloat16 on the way count: a program that leaves them out, or rounds other values in their place, can miss the bound.
Values may be sent and summed in bfloat16 or wider, within the bound.
A program may use at most 192 MiB of HBM per device.

v0:
```python
import jax
import jax.numpy as jnp
from jax import lax
from jax.sharding import PartitionSpec as P

HEAD_DIM = 64


def matmul(left_side, right_side):
    return jnp.dot(left_side, right_side, preferred_element_type=jnp.float32)


def outer_sum(left_side, right_side):
    return lax.dot_general(
        left_side, right_side, (((0,), (0,)), ((), ())), preferred_element_type=jnp.float32
    )


def back_matmul(left_side, right_side):
    return lax.dot_general(
        left_side, right_side, (((1,), (1,)), ((), ())), preferred_element_type=jnp.float32
    )


def column_sums(operand):
    return jnp.sum(operand.astype(jnp.float32), axis=0)


def gather_features(operand):
    return lax.all_gather(operand, "col", axis=1, tiled=True)


def sum_rows_out(partial_value):
    return lax.psum_scatter(partial_value, "row", scatter_dimension=0, tiled=True)


def sum_keys(first_part, second_part):
    return lax.psum((first_part, second_part), "row")


def gather_rows(operand):
    return lax.all_gather(operand, "row", axis=0, tiled=True)


def sum_features(partial_value):
    return lax.psum_scatter(partial_value, "col", scatter_dimension=1, tiled=True)


def gather_grad_features(operand):
    return lax.all_gather(operand, "col", axis=1, tiled=True)


def sum_grad_rows(partial_value):
    return lax.psum_scatter(
        partial_value.astype(jnp.bfloat16), "row", scatter_dimension=0, tiled=True
    ).astype(jnp.float32)


def gather_grad_rows(operand):
    return lax.all_gather(operand, "row", axis=0, tiled=True)


def sum_grad_keys(first_part, second_part):
    return (
        lax.psum(first_part.astype(jnp.bfloat16), "row").astype(jnp.float32),
        lax.psum(second_part.astype(jnp.bfloat16), "row").astype(jnp.float32),
    )


def sum_grad_features(partial_value):
    return lax.psum_scatter(
        partial_value.astype(jnp.bfloat16), "col", scatter_dimension=1, tiled=True
    ).astype(jnp.float32)


def attention_scores(queries, key_block, allowed, heads_here):
    query_heads = queries.reshape(queries.shape[0], heads_here, HEAD_DIM)
    key_heads = key_block.reshape(key_block.shape[0], heads_here, HEAD_DIM)
    scores = jnp.einsum(
        "qhd,khd->hqk", query_heads, key_heads, preferred_element_type=jnp.float32
    ) * HEAD_DIM ** (-0.5)
    if allowed is None:
        return scores
    return jnp.where(allowed[None], scores, -1e30)


def attention_forward(queries, key_block, value_block, allowed, heads_here):
    scores = attention_scores(queries, key_block, allowed, heads_here)
    row_top = jnp.max(scores, axis=-1, keepdims=True)
    raw_weights = jnp.exp(scores - row_top)
    exp_total = jnp.sum(raw_weights, axis=-1, keepdims=True)
    attn_probs = raw_weights / exp_total
    log_total = row_top + jnp.log(exp_total)
    value_heads = value_block.reshape(value_block.shape[0], heads_here, HEAD_DIM)
    mixed = jnp.einsum(
        "hqk,khd->qhd",
        attn_probs.astype(jnp.bfloat16),
        value_heads,
        preferred_element_type=jnp.float32,
    )
    return (
        mixed.reshape(queries.shape[0], heads_here * HEAD_DIM).astype(jnp.bfloat16),
        attn_probs,
        log_total,
    )


def attention_backward(queries, key_block, value_block, allowed, heads_here, log_total, grad_mixed):
    attn_probs = jnp.exp(attention_scores(queries, key_block, allowed, heads_here) - log_total)
    query_rows = queries.shape[0]
    key_count = key_block.shape[0]
    query_heads = queries.reshape(query_rows, heads_here, HEAD_DIM)
    key_heads = key_block.reshape(key_count, heads_here, HEAD_DIM)
    value_heads = value_block.reshape(key_count, heads_here, HEAD_DIM)
    grad_heads = grad_mixed.reshape(query_rows, heads_here, HEAD_DIM)
    grad_probs = jnp.einsum(
        "qhd,khd->hqk", grad_heads, value_heads, preferred_element_type=jnp.float32
    )
    row_delta = jnp.sum(grad_probs * attn_probs, axis=-1, keepdims=True)
    grad_scores = (attn_probs * (grad_probs - row_delta)).astype(jnp.bfloat16)
    score_scale = HEAD_DIM ** (-0.5)
    grad_queries = (
        jnp.einsum("hqk,khd->qhd", grad_scores, key_heads, preferred_element_type=jnp.float32)
        * score_scale
    )
    grad_keys = (
        jnp.einsum("hqk,qhd->khd", grad_scores, query_heads, preferred_element_type=jnp.float32)
        * score_scale
    )
    grad_values = jnp.einsum(
        "hqk,qhd->khd",
        attn_probs.astype(jnp.bfloat16),
        grad_heads,
        preferred_element_type=jnp.float32,
    )
    feature_count = heads_here * HEAD_DIM
    return (
        grad_queries.reshape(query_rows, feature_count).astype(jnp.bfloat16),
        grad_keys.reshape(key_count, feature_count),
        grad_values.reshape(key_count, feature_count),
    )


def shards(
    inputs,
    memory,
    teacher,
    segment_ids,
    parent_ids,
    valid_length,
    query_weight,
    query_bias,
    key_weight,
    value_weight,
    value_bias,
    proj_weight,
    proj_bias,
    cross_query_weight,
    cross_query_bias,
    cross_key_weight,
    cross_value_weight,
    cross_value_bias,
    cross_proj_weight,
    cross_proj_bias,
    up_weight,
    up_bias,
    down_weight,
    down_bias,
):
    tree_rows = inputs.shape[0]
    col_piece = inputs.shape[1]
    row_index = lax.axis_index("row")
    col_index = lax.axis_index("col")
    rows_mine = tree_rows // lax.axis_size("row")
    heads_here = query_weight.shape[1] // HEAD_DIM
    own_start = col_index * col_piece
    row_start = row_index * rows_mine
    row_pos = row_start + jnp.arange(rows_mine, dtype=jnp.int32)
    key_pos = jnp.arange(tree_rows, dtype=jnp.int32)
    seg_rows = lax.dynamic_slice_in_dim(segment_ids, row_start, rows_mine)
    par_rows = lax.dynamic_slice_in_dim(parent_ids, row_start, rows_mine)
    relation = (
        (segment_ids[None, :] == seg_rows[:, None])
        | (segment_ids[None, :] == par_rows[:, None])
        | (segment_ids[None, :] == 0)
    )
    allowed = (key_pos[None, :] <= row_pos[:, None]) & relation
    input_cols = gather_features(inputs)
    memory_cols = gather_features(memory)
    queries = (sum_rows_out(matmul(input_cols, query_weight)) + query_bias).astype(jnp.bfloat16)
    key_sum, value_sum = sum_keys(matmul(input_cols, key_weight), matmul(input_cols, value_weight))
    key_rows = key_sum.astype(jnp.bfloat16)
    value_rows = (value_sum + value_bias).astype(jnp.bfloat16)
    attention, self_probs, self_log = attention_forward(
        queries, key_rows, value_rows, allowed, heads_here
    )
    attention_rows = gather_rows(attention)
    proj_part = matmul(attention_rows, proj_weight)
    hidden_one = (
        inputs.astype(jnp.float32)
        + sum_features(proj_part)
        + lax.dynamic_slice_in_dim(proj_bias, own_start, col_piece)
    )
    hidden_one_cols = gather_features(hidden_one.astype(jnp.bfloat16))
    cross_queries = (
        sum_rows_out(matmul(hidden_one_cols, cross_query_weight)) + cross_query_bias
    ).astype(jnp.bfloat16)
    cross_key_sum, cross_value_sum = sum_keys(
        matmul(memory_cols, cross_key_weight), matmul(memory_cols, cross_value_weight)
    )
    cross_keys = cross_key_sum.astype(jnp.bfloat16)
    cross_values = (cross_value_sum + cross_value_bias).astype(jnp.bfloat16)
    cross_out, cross_probs, cross_log = attention_forward(
        cross_queries, cross_keys, cross_values, None, heads_here
    )
    cross_out_rows = gather_rows(cross_out)
    cross_part = matmul(cross_out_rows, cross_proj_weight)
    hidden_two = (
        hidden_one
        + sum_features(cross_part)
        + lax.dynamic_slice_in_dim(cross_proj_bias, own_start, col_piece)
    )
    hidden_two_cols = gather_features(hidden_two.astype(jnp.bfloat16))
    upper = sum_rows_out(matmul(hidden_two_cols, up_weight)) + up_bias
    active = jnp.where(upper > 0, upper, 0.0).astype(jnp.bfloat16)
    active_rows = gather_rows(active)
    result = (
        hidden_two
        + sum_features(matmul(active_rows, down_weight))
        + lax.dynamic_slice_in_dim(down_bias, own_start, col_piece)
    )
    output = result.astype(jnp.bfloat16)
    valid_rows = (key_pos < valid_length[0]).astype(jnp.float32)[:, None]
    difference = result - teacher.astype(jnp.float32)
    square_part = jnp.sum(valid_rows * difference * difference)
    first_device = ((row_index == 0) & (col_index == 0)).astype(jnp.float32)
    count_part = valid_length[0].astype(jnp.float32) * first_device
    square_total, count_total = lax.psum((square_part, count_part), ("dp", "row", "col"))
    mean_loss = 0.5 * square_total / count_total
    loss_factor = float(lax.axis_size("dp") * tree_rows)
    grad_result = loss_factor / count_total * valid_rows * difference
    grad_out_cols = gather_grad_features(grad_result.astype(jnp.bfloat16))
    grad_down_weight = outer_sum(active_rows, grad_out_cols)
    grad_down_bias = column_sums(grad_out_cols)
    grad_active = sum_grad_rows(back_matmul(grad_out_cols, down_weight)).astype(jnp.bfloat16)
    grad_upper = jnp.where(upper > 0, grad_active, jnp.zeros_like(grad_active))
    grad_upper_rows = gather_grad_rows(grad_upper)
    grad_up_weight = outer_sum(hidden_two_cols, grad_upper_rows)
    grad_up_bias = column_sums(grad_upper_rows)
    grad_two = grad_result + sum_grad_features(back_matmul(grad_upper_rows, up_weight))
    grad_cross_cols = gather_grad_features(grad_two.astype(jnp.bfloat16))
    grad_cross_proj_weight = outer_sum(cross_out_rows, grad_cross_cols)
    grad_cross_proj_bias = column_sums(grad_cross_cols)
    grad_cross_out = sum_grad_rows(back_matmul(grad_cross_cols, cross_proj_weight)).astype(
        jnp.bfloat16
    )
    grad_cross_queries, cross_key_part, cross_value_part = attention_backward(
        cross_queries, cross_keys, cross_values, None, heads_here, cross_log, grad_cross_out
    )
    cross_key_total, cross_value_total = sum_grad_keys(cross_key_part, cross_value_part)
    grad_cross_keys = cross_key_total.astype(jnp.bfloat16)
    grad_cross_values = cross_value_total.astype(jnp.bfloat16)
    grad_cross_query_rows = gather_grad_rows(grad_cross_queries)
    grad_cross_query_weight = outer_sum(hidden_one_cols, grad_cross_query_rows)
    grad_cross_query_bias = column_sums(grad_cross_query_rows)
    grad_cross_key_weight = outer_sum(memory_cols, grad_cross_keys)
    grad_cross_value_weight = outer_sum(memory_cols, grad_cross_values)
    grad_cross_value_bias = column_sums(grad_cross_values)
    grad_memory = sum_grad_features(
        back_matmul(grad_cross_keys, cross_key_weight)
        + back_matmul(grad_cross_values, cross_value_weight)
    )
    grad_one = grad_two + sum_grad_features(back_matmul(grad_cross_query_rows, cross_query_weight))
    grad_branch_cols = gather_grad_features(grad_one.astype(jnp.bfloat16))
    grad_proj_weight = outer_sum(attention_rows, grad_branch_cols)
    grad_proj_bias = column_sums(grad_branch_cols)
    grad_attention = sum_grad_rows(back_matmul(grad_branch_cols, proj_weight)).astype(jnp.bfloat16)
    grad_queries, self_key_part, self_value_part = attention_backward(
        queries, key_rows, value_rows, allowed, heads_here, self_log, grad_attention
    )
    self_key_total, self_value_total = sum_grad_keys(self_key_part, self_value_part)
    grad_keys = self_key_total.astype(jnp.bfloat16)
    grad_values = self_value_total.astype(jnp.bfloat16)
    grad_query_rows = gather_grad_rows(grad_queries)
    grad_query_weight = outer_sum(input_cols, grad_query_rows)
    grad_query_bias = column_sums(grad_query_rows)
    grad_key_weight = outer_sum(input_cols, grad_keys)
    grad_value_weight = outer_sum(input_cols, grad_values)
    grad_value_bias = column_sums(grad_values)
    input_part = (
        back_matmul(grad_query_rows, query_weight)
        + back_matmul(grad_keys, key_weight)
        + back_matmul(grad_values, value_weight)
    )
    grad_input = grad_one + sum_grad_features(input_part)
    totals = (
        lax.psum(grad_query_weight.astype(jnp.bfloat16), "dp").astype(jnp.float32),
        lax.psum(grad_query_bias.astype(jnp.bfloat16), "dp").astype(jnp.float32),
        lax.psum(grad_key_weight.astype(jnp.bfloat16), "dp").astype(jnp.float32),
        lax.psum(grad_value_weight.astype(jnp.bfloat16), "dp").astype(jnp.float32),
        lax.psum(grad_value_bias.astype(jnp.bfloat16), "dp").astype(jnp.float32),
        lax.psum(grad_proj_weight.astype(jnp.bfloat16), "dp").astype(jnp.float32),
        lax.psum(grad_proj_bias.astype(jnp.bfloat16), "dp").astype(jnp.float32),
        lax.psum(grad_cross_query_weight.astype(jnp.bfloat16), "dp").astype(jnp.float32),
        lax.psum(grad_cross_query_bias.astype(jnp.bfloat16), "dp").astype(jnp.float32),
        lax.psum(grad_cross_key_weight.astype(jnp.bfloat16), "dp").astype(jnp.float32),
        lax.psum(grad_cross_value_weight.astype(jnp.bfloat16), "dp").astype(jnp.float32),
        lax.psum(grad_cross_value_bias.astype(jnp.bfloat16), "dp").astype(jnp.float32),
        lax.psum(grad_cross_proj_weight.astype(jnp.bfloat16), "dp").astype(jnp.float32),
        lax.psum(grad_cross_proj_bias.astype(jnp.bfloat16), "dp").astype(jnp.float32),
        lax.psum(grad_up_weight.astype(jnp.bfloat16), "dp").astype(jnp.float32),
        lax.psum(grad_up_bias.astype(jnp.bfloat16), "dp").astype(jnp.float32),
        lax.psum(grad_down_weight.astype(jnp.bfloat16), "dp").astype(jnp.float32),
        lax.psum(grad_down_bias.astype(jnp.bfloat16), "dp").astype(jnp.float32),
    )
    return (
        output,
        mean_loss,
        grad_input,
        grad_memory,
        totals[0],
        totals[1],
        totals[2],
        totals[3],
        totals[4],
        totals[5],
        totals[6],
        totals[7],
        totals[8],
        totals[9],
        totals[10],
        totals[11],
        totals[12],
        totals[13],
        totals[14],
        totals[15],
        totals[16],
        totals[17],
    )


def solution(mesh):
    in_specs = (
        P("dp", ("row", "col")),
        P("dp", ("row", "col")),
        P("dp", ("row", "col")),
        P("dp"),
        P("dp"),
        P("dp"),
        P("row", "col"),
        P("col"),
        P("row", "col"),
        P("row", "col"),
        P("col"),
        P("col", "row"),
        P("row"),
        P("row", "col"),
        P("col"),
        P("row", "col"),
        P("row", "col"),
        P("col"),
        P("col", "row"),
        P("row"),
        P("row", "col"),
        P("col"),
        P("col", "row"),
        P("row"),
    )
    out_specs = (
        P("dp", ("row", "col")),
        P(),
        P("dp", ("row", "col")),
        P("dp", ("row", "col")),
        P("row", "col"),
        P("col"),
        P("row", "col"),
        P("row", "col"),
        P("col"),
        P("col", "row"),
        P("row"),
        P("row", "col"),
        P("col"),
        P("row", "col"),
        P("row", "col"),
        P("col"),
        P("col", "row"),
        P("row"),
        P("row", "col"),
        P("col"),
        P("col", "row"),
        P("row"),
    )
    return jax.shard_map(shards, mesh=mesh, in_specs=in_specs, out_specs=out_specs, check_vma=False)
```

profile of v0, /device:TPU:0, one launch (start us, length us, event | category | flops | bytes accessed | tf_op | source)
XLA Modules:
  0.0 1382.1 jit_solution(2587529920620217880)
XLA Ops:
  59.3 133.5 %all-reduce.19 = (bf16[4096,128]{1,0:T(8,128)(2,1)}, bf16[1024,128]{1,0:T(8,128)(2,1)}) all-reduce(f32[4096,128]{1,0:T(8,128)S(1)} %fusion.44, f32[1024,128]{1,0:T(8,128)} %fusion.48), channel_id=1, replica_groups=mesh['dp'=2,'row'=4,'col'=4] {'row'}, use_global_device_ids=true, to_apply=%region_2.0 | all-reduce | flops 655360 | bytes 3932160 | tf_op jit(solution)/shard_map/psum | solution.py:38
  248.8 26.7 %all-gather.15.cloned.1.call-done = bf16[4096,128]{0,1:T(8,128)(2,1)} async-done(((bf16[1024,128]{0,1:T(8,128)(2,1)}), bf16[4096,128]{0,1:T(8,128)(2,1)}) %all-gather.15.cloned.1.call-update) | async-done | bytes 1048592 | tf_op jit(solution)/shard_map/all_gather | solution.py:42
  278.6 43.9 %reduce-scatter.16.cloned.1.call-done = f32[4096,32]{0,1:T(8,128)} async-done(((f32[4096,128]{0,1:T(8,128)}), f32[4096,32]{0,1:T(8,128)}) %reduce-scatter.16.cloned.1.call-update) | async-done | bytes 524304 | tf_op jit(solution)/shard_map/reduce_scatter | solution.py:46
  324.4 27.4 %all-gather.17.cloned.1.call-done = bf16[4096,128]{0,1:T(8,128)(2,1)} async-done(((bf16[4096,32]{0,1:T(8,128)(2,1)}), bf16[4096,128]{0,1:T(8,128)(2,1)}) %all-gather.17.cloned.1.call-update) | async-done | bytes 1048592 | tf_op jit(solution)/shard_map/all_gather | solution.py:30
  355.5 34.3 %reduce-scatter.18.cloned.1.call-done = f32[1024,128]{1,0:T(8,128)} async-done(((f32[4096,128]{1,0:T(8,128)}), f32[1024,128]{1,0:T(8,128)}) %reduce-scatter.18.cloned.1.call-update) | async-done | bytes 524304 | tf_op jit(solution)/shard_map/reduce_scatter | solution.py:34
  396.4 26.7 %all-gather.19.cloned.1.call-done = bf16[4096,128]{0,1:T(8,128)(2,1)} async-done(((bf16[1024,128]{0,1:T(8,128)(2,1)}), bf16[4096,128]{0,1:T(8,128)(2,1)}) %all-gather.19.cloned.1.call-update) | async-done | bytes 1048592 | tf_op jit(solution)/shard_map/all_gather | solution.py:42
  426.3 43.9 %reduce-scatter.20.cloned.1.call-done = f32[4096,32]{0,1:T(8,128)} async-done(((f32[4096,128]{0,1:T(8,128)}), f32[4096,32]{0,1:T(8,128)}) %reduce-scatter.20.cloned.1.call-update) | async-done | bytes 524304 | tf_op jit(solution)/shard_map/reduce_scatter | solution.py:46
  472.2 27.4 %all-gather.21.cloned.1.call-done = bf16[4096,128]{0,1:T(8,128)(2,1)} async-done(((bf16[4096,32]{0,1:T(8,128)(2,1)}), bf16[4096,128]{0,1:T(8,128)(2,1)}) %all-gather.21.cloned.1.call-update) | async-done | bytes 1048592 | tf_op jit(solution)/shard_map/all_gather | solution.py:30
  505.5 86.0 %reduce-scatter.22.cloned.1.call-done = f32[1024,512]{1,0:T(8,128)} async-done(((f32[4096,512]{1,0:T(8,128)}), f32[1024,512]{1,0:T(8,128)}) %reduce-scatter.22.cloned.1.call-update) | async-done | bytes 2097168 | tf_op jit(solution)/shard_map/reduce_scatter | solution.py:34
  594.4 52.8 %all-gather.23.cloned.1.call-done = bf16[4096,512]{1,0:T(8,128)(2,1)} async-done(((bf16[1024,512]{1,0:T(8,128)(2,1)}), bf16[4096,512]{1,0:T(8,128)(2,1)}) %all-gather.23.cloned.1.call-update) | async-done | bytes 4194320 | tf_op jit(solution)/shard_map/all_gather | solution.py:42
  653.6 42.7 %reduce-scatter.24.cloned.1.call-done = f32[4096,32]{0,1:T(8,128)} async-done(((f32[4096,128]{0,1:T(8,128)}), f32[4096,32]{0,1:T(8,128)}) %reduce-scatter.24.cloned.1.call-update) | async-done | bytes 524304 | tf_op jit(solution)/shard_map/reduce_scatter | solution.py:46
  698.5 39.8 %all-reduce = (f32[]{:T(128)}, f32[]{:T(128)}) all-reduce(f32[]{:T(128)S(6)} %mul.82, f32[]{:T(128)} %get-tuple-element.96), channel_id=1, replica_groups=mesh['dp'=2,'row'=4,'col'=4] {'dp','row','col'}, use_global_device_ids=true, to_apply=%region_16.17 | all-reduce | flops 2 | bytes 16 | tf_op jit(solution)/shard_map/psum | solution.py:238
  740.8 28.0 %all-gather.25.cloned.1.call-done = bf16[4096,128]{0,1:T(8,128)(2,1)} async-done(((bf16[4096,32]{0,1:T(8,128)(2,1)}), bf16[4096,128]{0,1:T(8,128)(2,1)}) %all-gather.25.cloned.1.call-update) | async-done | bytes 1048592 | tf_op jit(solution)/shard_map/all_gather | solution.py:50
  773.5 52.3 %reduce-scatter.26.cloned.1.call-done = bf16[1024,512]{1,0:T(8,128)(2,1)} async-done(((bf16[4096,512]{1,0:T(8,128)(2,1)}), bf16[1024,512]{1,0:T(8,128)(2,1)}) %reduce-scatter.26.cloned.1.call-update) | async-done | bytes 1048592 | tf_op jit(solution)/shard_map/reduce_scatter | solution.py:54
  828.4 52.8 %all-gather.27.cloned.1.call-done = bf16[4096,512]{1,0:T(8,128)(2,1)} async-done(((bf16[1024,512]{1,0:T(8,128)(2,1)}), bf16[4096,512]{1,0:T(8,128)(2,1)}) %all-gather.27.cloned.1.call-update) | async-done | bytes 4194320 | tf_op jit(solution)/shard_map/all_gather | solution.py:60
  886.4 26.8 %reduce-scatter.28.cloned.1.call-done = bf16[4096,32]{0,1:T(8,128)(2,1)} async-done(((bf16[4096,128]{0,1:T(8,128)(2,1)}), bf16[4096,32]{0,1:T(8,128)(2,1)}) %reduce-scatter.28.cloned.1.call-update) | async-done | bytes 262160 | tf_op jit(solution)/shard_map/reduce_scatter | solution.py:71
  915.2 26.8 %all-gather.29.cloned.1.call-done = bf16[4096,128]{0,1:T(8,128)(2,1)} async-done(((bf16[4096,32]{0,1:T(8,128)(2,1)}), bf16[4096,128]{0,1:T(8,128)(2,1)}) %all-gather.29.cloned.1.call-update) | async-done | bytes 1048592 | tf_op jit(solution)/shard_map/all_gather | solution.py:50
  944.8 27.6 %reduce-scatter.30.cloned.1.call-done = bf16[1024,128]{1,0:T(8,128)(2,1)} async-done(((bf16[4096,128]{1,0:T(8,128)(2,1)}), bf16[1024,128]{1,0:T(8,128)(2,1)}) %reduce-scatter.30.cloned.1.call-update) | async-done | bytes 262160 | tf_op jit(solution)/shard_map/reduce_scatter | solution.py:54
  986.3 26.7 %all-gather.31.cloned.1.call-done = bf16[4096,128]{0,1:T(8,128)(2,1)} async-done(((bf16[1024,128]{0,1:T(8,128)(2,1)}), bf16[4096,128]{0,1:T(8,128)(2,1)}) %all-gather.31.cloned.1.call-update) | async-done | bytes 1048592 | tf_op jit(solution)/shard_map/all_gather | solution.py:60
  1015.8 27.3 %reduce-scatter.32.cloned.1.call-done = bf16[4096,32]{0,1:T(8,128)(2,1)} async-done(((bf16[4096,128]{0,1:T(8,128)(2,1)}), bf16[4096,32]{0,1:T(8,128)(2,1)}) %reduce-scatter.32.cloned.1.call-update) | async-done | bytes 262160 | tf_op jit(solution)/shard_map/reduce_scatter | solution.py:71
  1044.9 27.1 %all-gather.33.cloned.1.call-done = bf16[4096,128]{0,1:T(8,128)(2,1)} async-done(((bf16[4096,32]{0,1:T(8,128)(2,1)}), bf16[4096,128]{0,1:T(8,128)(2,1)}) %all-gather.33.cloned.1.call-update) | async-done | bytes 1048592 | tf_op jit(solution)/shard_map/all_gather | solution.py:50
  1125.4 27.5 %multiply_convert_fusion = bf16[2,1024,4096]{2,1,0:T(8,128)(2,1)} fusion(f32[2,1024,4096]{2,1,0:T(8,128)} %get-tuple-element.106, f32[2,1024,4096]{2,1,0:T(8,128)} %get-tuple-element.100, f32[2,1024]{1,0:T(2,128)S(1)} %get-tuple-element.105, f32[2,1024]{1,0:T(2,128)S(1)} %log_add_fusion), kind=kLoop, calls=%fused_computation | loop fusion | flops 33554432 | bytes 83902464 | tf_op jit(solution)/shard_map/convert_element_type | solution.py:120
  1219.8 54.6 %all-reduce.14.cloned.1.call-done = (bf16[4096,128]{0,1:T(8,128)(2,1)}, bf16[4096,128]{0,1:T(8,128)(2,1)}, bf16[1024,128]{0,1:T(8,128)(2,1)}, bf16[1024,128]{0,1:T(8,128)(2,1)}) async-done(((bf16[4096,128]{0,1:T(8,128)(2,1)}, bf16[4096,128]{0,1:T(8,128)(2,1)}, bf16[1024,128]{0,1:T(8,128)(2,1)}, bf16[1024,128]{0,1:T(8,128)(2,1)}), (bf16[4096,128]{0,1:T(8,128)(2,1)}, bf16[4096,128]{0,1:T(8,128)(2,1)}, ...) | async-done | bytes 2621456 | tf_op jit(solution)/shard_map/psum | solution.py:65
  1346.2 26.3 %reduce-scatter.36.cloned.1.call-done = bf16[4096,32]{0,1:T(8,128)(2,1)} async-done(((bf16[4096,128]{0,1:T(8,128)(2,1)}), bf16[4096,32]{0,1:T(8,128)(2,1)}) %reduce-scatter.36.cloned.1.call-update) | async-done | bytes 262160 | tf_op jit(solution)/shard_map/reduce_scatter | solution.py:71
  (303 shorter events, 374.5 us)
Async XLA Ops:
  8.0 186.4 %all-reduce.12.cloned.1.call-start = ((), (), s32[]{:S(2)}) async-start(), calls=%async_computation.38 | async-start | bytes 5242880 | tf_op jit(solution)/shard_map/psum | solution.py:38
  44.4 158.6 %reduce-scatter.14.cloned.1.call-start = ((), (), s32[]{:S(2)}) async-start(), calls=%async_computation.14 | async-start | bytes 2621440 | tf_op jit(solution)/shard_map/reduce_scatter | solution.py:34
  50.3 225.1 %all-gather.15.cloned.1.call-start = ((), (), s32[]{:S(2)}) async-start(), calls=%async_computation.15 | async-start | bytes 1310720 | tf_op jit(solution)/shard_map/all_gather | solution.py:42
  248.7 73.8 %reduce-scatter.16.cloned.1.call-start = ((), (), s32[]{:S(2)}) async-start(), calls=%async_computation.16 | async-start | bytes 2621440 | tf_op jit(solution)/shard_map/reduce_scatter | solution.py:46
  278.5 73.4 %all-gather.17.cloned.1.call-start = ((), (), s32[]{:S(2)}) async-start(), calls=%async_computation.17 | async-start | bytes 1310720 | tf_op jit(solution)/shard_map/all_gather | solution.py:30
  324.4 65.5 %reduce-scatter.18.cloned.1.call-start = ((), (), s32[]{:S(2)}) async-start(), calls=%async_computation.18 | async-start | bytes 2621440 | tf_op jit(solution)/shard_map/reduce_scatter | solution.py:34
  354.9 68.2 %all-gather.19.cloned.1.call-start = ((), (), s32[]{:S(2)}) async-start(), calls=%async_computation.19 | async-start | bytes 1310720 | tf_op jit(solution)/shard_map/all_gather | solution.py:42
  396.4 73.8 %reduce-scatter.20.cloned.1.call-start = ((), (), s32[]{:S(2)}) async-start(), calls=%async_computation.20 | async-start | bytes 2621440 | tf_op jit(solution)/shard_map/reduce_scatter | solution.py:46
  426.2 73.4 %all-gather.21.cloned.1.call-start = ((), (), s32[]{:S(2)}) async-start(), calls=%async_computation.21 | async-start | bytes 1310720 | tf_op jit(solution)/shard_map/all_gather | solution.py:30
  472.1 119.3 %reduce-scatter.22.cloned.1.call-start = ((), (), s32[]{:S(2)}) async-start(), calls=%async_computation.22 | async-start | bytes 10485760 | tf_op jit(solution)/shard_map/reduce_scatter | solution.py:34
  505.4 141.8 %all-gather.23.cloned.1.call-start = ((), (), s32[]{:S(2)}) async-start(), calls=%async_computation.23 | async-start | bytes 5242880 | tf_op jit(solution)/shard_map/all_gather | solution.py:42
  594.4 101.9 %reduce-scatter.24.cloned.1.call-start = ((), (), s32[]{:S(2)}) async-start(), calls=%async_computation.24 | async-start | bytes 2621440 | tf_op jit(solution)/shard_map/reduce_scatter | solution.py:46
  652.3 116.5 %all-gather.25.cloned.1.call-start = ((), (), s32[]{:S(2)}) async-start(), calls=%async_computation.25 | async-start | bytes 1310720 | tf_op jit(solution)/shard_map/all_gather | solution.py:50
  740.8 85.0 %reduce-scatter.26.cloned.1.call-start = ((), (), s32[]{:S(2)}) async-start(), calls=%async_computation.26 | async-start | bytes 5242880 | tf_op jit(solution)/shard_map/reduce_scatter | solution.py:54
  773.4 107.8 %all-gather.27.cloned.1.call-start = ((), (), s32[]{:S(2)}) async-start(), calls=%async_computation.27 | async-start | bytes 5242880 | tf_op jit(solution)/shard_map/all_gather | solution.py:60
  828.4 84.9 %reduce-scatter.28.cloned.1.call-start = ((), (), s32[]{:S(2)}) async-start(), calls=%async_computation.28 | async-start | bytes 1310720 | tf_op jit(solution)/shard_map/reduce_scatter | solution.py:71
  944.7 68.4 %all-gather.31.cloned.1.call-start = ((), (), s32[]{:S(2)}) async-start(), calls=%async_computation.31 | async-start | bytes 1310720 | tf_op jit(solution)/shard_map/all_gather | solution.py:60
  1044.8 57.5 %reduce-scatter.34.cloned.1.call-start = ((), (), s32[]{:S(2)}) async-start(), calls=%async_computation.34 | async-start | bytes 1310720 | tf_op jit(solution)/shard_map/reduce_scatter | solution.py:54
  1074.6 137.9 %all-gather.35.cloned.1.call-start = ((), (), s32[]{:S(2)}) async-start(), calls=%async_computation.35 | async-start | bytes 1310720 | tf_op jit(solution)/shard_map/all_gather | solution.py:60
  1164.6 109.8 %all-reduce.14.cloned.1.call-start = ((), (), s32[]{:S(2)}) async-start(), calls=%async_computation.39 | async-start | bytes 5242880 | tf_op jit(solution)/shard_map/psum | solution.py:65
  1189.3 106.3 %all-reduce.18.cloned.1.call-start = ((), (), s32[]{:S(2)}) async-start(), calls=%async_computation.41 | async-start | bytes 524288 | tf_op jit(solution)/shard_map/psum | solution.py:311
  1198.3 123.3 %all-reduce.16.cloned.1.call-start = ((), (), s32[]{:S(2)}) async-start(), calls=%async_computation.40 | async-start | bytes 533504 | tf_op jit(solution)/shard_map/psum | solution.py:297
  1286.3 58.4 %reduce-scatter.38.cloned.1.call-start = ((), (), s32[]{:S(2)}) async-start(), calls=%async_computation.37 | async-start | bytes 327680 | tf_op jit(solution)/shard_map/reduce_scatter | solution.py:71
  1289.4 83.0 %reduce-scatter.36.cloned.1.call-start = ((), (), s32[]{:S(2)}) async-start(), calls=%async_computation.36 | async-start | bytes 1310720 | tf_op jit(solution)/shard_map/reduce_scatter | solution.py:71
  (68 other events, 5012.7 us)
Sparse Core Ops, SparseCore 0:
  9.6 31.5 all-gather.12
  45.0 108.1 all-reduce.11
  156.4 46.5 reduce-scatter.13
  248.8 26.5 all-gather.14
  278.6 43.8 reduce-scatter.15
  324.6 27.2 all-gather.16
  355.1 34.6 reduce-scatter.17
  396.5 26.5 all-gather.18
  426.3 43.8 reduce-scatter.19
  472.3 27.2 all-gather.20
  505.5 85.9 reduce-scatter.21
  594.5 52.6 all-gather.22
  652.4 43.8 reduce-scatter.23
  740.9 27.9 all-gather.24
  773.5 52.1 reduce-scatter.25
  828.5 52.6 all-gather.26
  886.1 27.1 reduce-scatter.27
  915.3 26.5 all-gather.28
  945.1 27.2 reduce-scatter.29
  986.4 26.6 all-gather.30
  1015.9 27.1 reduce-scatter.31
  1075.1 27.2 reduce-scatter.33
  1164.7 26.6 all-gather.34
  1195.4 78.9 all-reduce.13
  (5 shorter events, 111.8 us)
where the time goes:
time: 1390 us; the launch traced here: 1380 us
  waiting for transfers between devices  853 us (61%)
  matrix products  191 us (14%)
  blocking collectives  190 us (14%)
  other arithmetic  111 us (8%)
  between operations  19 us (1%)
  local copies, waits for them, and re-layouts  15.9 us (1%)
    psum x1, blocking collectives, sum_keys(): return lax.psum((first_part, second_part), 'row')  134 us
    reduce_scatter x3, waiting for transfers between devices, sum_features(): lax.psum_scatter(partial_value, 'col', scatter_dimension=1, tiled=True)  130 us
    reduce_scatter x3, waiting for transfers between devices, sum_rows_out(): lax.psum_scatter(partial_value, 'row', scatter_dimension=0, tiled=True)  126 us
    all_gather x3, waiting for transfers between devices, gather_rows(): return lax.all_gather(operand, 'row', axis=0, tiled=True)  106 us
    reduce_scatter x3, waiting for transfers between devices, sum_grad_rows(): lax.psum_scatter(partial_value.astype(jnp.bfloat16), 'row', scatter_dimen...  97.3 us
    reduce_scatter x4, waiting for transfers between devices, sum_grad_features(): lax.psum_scatter(partial_value.astype(jnp.bfloat16), 'col', scatter_dimen...  82.5 us
    all_gather x3, waiting for transfers between devices, gather_grad_features(): return lax.all_gather(operand, 'col', axis=1, tiled=True)  81.9 us
    all_gather x3, waiting for transfers between devices, gather_grad_rows(): return lax.all_gather(operand, 'row', axis=0, tiled=True)  79.6 us
  transfers between devices with their start and end apart: 29, of which 27 were waited for; matrix products, arithmetic and copies ran while one was open for 9% of the time, Pallas kernels for 0%

commit v1 on v0

v1 whole, which is shorter than its diff:
```python
import functools

import jax
import jax.numpy as jnp
from jax import lax
from jax.experimental import pallas as pl
from jax.experimental.pallas import tpu as pltpu
from jax.sharding import PartitionSpec as P

HEAD_DIM = 64
HEADS = 8
MASKED = -1e30
BF16 = jnp.bfloat16
F32 = jnp.float32
MESH = pl.DeviceIdType.MESH
DMA = pltpu.SemaphoreType.DMA
VMEM_LIMIT = 56 * 2**20


def mm(a, b):
    return jnp.dot(a, b, preferred_element_type=F32)


def mm_nt(a, b):
    return lax.dot_general(a, b, (((1,), (1,)), ((), ())), preferred_element_type=F32)


def mm_tn(a, b):
    return lax.dot_general(a, b, (((0,), (0,)), ((), ())), preferred_element_type=F32)


def log2_of(size):
    return size.bit_length() - 1


class Place:
    def __init__(self, rows, cols):
        self.R, self.C = rows, cols
        self.G = rows * cols
        self.half = cols // 2
        self.P = self.G // 2
        self.per_head = self.P // HEADS
        self.S = 2 * self.per_head
        self.lr, self.lc = log2_of(rows), log2_of(cols)
        self.nb = self.lr + self.lc
        self.tdim = self.lr
        self.dims = [d for d in range(self.nb) if d != self.tdim]
        self.dp = lax.axis_index("dp")
        self.row = lax.axis_index("row")
        self.col = lax.axis_index("col")
        self.core = lax.rem(self.dp, 2)
        self.tree = self.col // self.half
        self.chip = self.row * cols + self.col
        self.p = self.row * self.half + lax.rem(self.col, self.half)
        self.head = self.p // self.per_head
        self.part = lax.rem(self.p, self.per_head) * 2 + self.core
        self.bits = [lax.rem(self.row // (1 << (self.lr - 1 - i)), 2) for i in range(self.lr)] + [
            lax.rem(self.col // (1 << (self.lc - 1 - i)), 2) for i in range(self.lc)
        ]
        self.base = self.dp - self.core

    def flip(self, dims, core=False):
        row, col, dp = self.row, self.col, self.dp
        for d in dims:
            if d < self.lr:
                row = row + (1 - 2 * self.bits[d]) * (1 << (self.lr - 1 - d))
            else:
                col = col + (1 - 2 * self.bits[d]) * (1 << (self.nb - 1 - d))
        if core:
            dp = dp + 1 - 2 * self.core
        return (dp, row, col)

    def masks(self, dims):
        return [[d for i, d in enumerate(dims) if m >> i & 1] for m in range(1 << len(dims))]

    def block_of(self, head, part):
        odd = lax.rem(head, 2)
        return head * self.S + part + odd * (self.S - 1 - 2 * part)

    def block_at(self, row, col, core):
        p = row * self.half + lax.rem(col, self.half)
        return self.block_of(p // self.per_head, lax.rem(p, self.per_head) * 2 + core)

    def device_of(self, head, part):
        p = head * self.per_head + part // 2
        return (self.base + lax.rem(part, 2), p // self.half, self.tree * self.half + lax.rem(p, self.half))

    def head_xor(self, m):
        other = self.head
        for i in range(log2_of(HEADS)):
            if m >> i & 1:
                other = other + (1 - 2 * lax.rem(self.head // (1 << i), 2)) * (1 << i)
        return other


def greet_all(me):
    barrier = pltpu.get_barrier_semaphore()
    count = 0
    for mask in me.masks(list(range(me.nb))):
        for core in (False, True):
            if mask or core:
                pl.semaphore_signal(barrier, inc=1, device_id=me.flip(mask, core), device_id_type=MESH)
                count += 1
    pl.semaphore_wait(barrier, count)


def send(src, dst, send_sem, recv_sem, to):
    return pltpu.make_async_remote_copy(
        src_ref=src, dst_ref=dst, send_sem=send_sem, recv_sem=recv_sem, device_id=to, device_id_type=MESH
    )


def aligned(index, size):
    return pl.multiple_of(index * size, size)


def when_not(condition):
    return pl.when(jnp.logical_not(condition))


def gather_kernel(
    R, C, TB, units, x_ref, t_ref, w_ref, x_out, t_out, w_out,
    fs, fr, ss, rs, cs, cr, ls, ts, tr, tl, ws, wr, wl,
):
    me = Place(R, C)
    greet_all(me)
    foreign = me.core != me.tree
    U = len(units)
    masks = me.masks(me.dims)
    piece = x_ref.shape[0]

    def lanes(u):
        return pl.ds(units[u][0], units[u][1])

    def own(u):
        index = list(me.bits)
        index[me.tdim] = me.core
        return tuple(index) + (slice(None), lanes(u))

    def far(u):
        return send(
            x_ref.at[:, lanes(u)], x_out.at[tuple(me.bits) + (slice(None), lanes(u))],
            fs.at[u], fr.at[u], me.flip([me.tdim], True),
        )

    def local(u):
        return pltpu.make_async_copy(x_ref.at[:, lanes(u)], x_out.at[own(u)], ls.at[u])

    def near(u, m):
        return send(x_out.at[own(u)], x_out.at[own(u)], ss.at[u, m], rs.at[u, m], me.flip(masks[m]))

    def across(u):
        index = [slice(None)] * me.nb
        index[me.tdim] = me.core
        index = tuple(index) + (slice(None), lanes(u))
        return send(x_out.at[index], x_out.at[index], cs.at[u], cr.at[u], me.flip([], True))

    w = w_ref.shape[1]
    heads_here = w // HEAD_DIM
    w_dst = w_out.at[:, :, pl.ds(aligned(me.row, 128), 128)]
    w_jobs = []
    for t in range(2):
        for i in range(heads_here):
            for j in range(me.per_head):
                p = (me.col * heads_here + i) * me.per_head + j
                to = (me.dp, p // me.half, t * me.half + lax.rem(p, me.half))
                to_me = (to[1] == me.row) & (to[2] == me.col)
                n = len(w_jobs)
                src = w_ref.at[:, pl.ds(i * HEAD_DIM, HEAD_DIM), :]
                w_jobs.append((
                    to_me,
                    pltpu.make_async_copy(src, w_dst, wl),
                    send(src, w_dst, ws.at[n], wr.at[me.row], to),
                ))
    for to_me, here, there in w_jobs:
        pl.when(to_me)(here.start)
        when_not(to_me)(there.start)

    @pl.when(foreign)
    def _():
        for u in range(U):
            far(u).start()
        for u in range(U):
            far(u).wait()
            for m in range(1, len(masks)):
                near(u, m).start()

    @when_not(foreign)
    def _():
        for u in range(U):
            local(u).start()
        for u in range(U):
            local(u).wait()
            for m in range(1, len(masks)):
                near(u, m).start()

    t_dst = t_out.at[me.chip]

    def t_job(m, c):
        mask = masks[m]
        away = me.flip(mask)
        row = away[1]
        col = lax.rem(away[2], me.half) + me.core * me.half
        core = me.core + c * (1 - 2 * me.core)
        block = me.block_at(row, col, core)
        src = t_ref.at[:, pl.ds(aligned(block, TB), TB)]
        to_me = jnp.logical_not(foreign) & (m + c == 0)
        there = send(src, t_dst, ts.at[m, c], tr.at[m, jnp.where(foreign, 1, 0)], (me.base + core, row, col))
        return to_me, pltpu.make_async_copy(src, t_dst, tl), there

    for m in range(len(masks)):
        for c in range(2):
            to_me, here, there = t_job(m, c)
            if m + c == 0:
                pl.when(to_me)(here.start)
                when_not(to_me)(there.start)
            else:
                there.start()

    for u in range(U):
        for m in range(1, len(masks)):
            near(u, m).wait_recv()
        across(u).start()
    for r in range(R):
        from_me = (me.row == r) & (me.head // heads_here == me.col)
        got = w_out.at[:, :, pl.ds(r * 128, 128)]
        pl.when(from_me)(pltpu.make_async_copy(got, got, wl).wait)
        when_not(from_me)(send(got, got, ws.at[0], wr.at[r], me.flip([], True)).wait_recv)
    for to_me, here, there in w_jobs:
        when_not(to_me)(there.wait_send)
    for m in range(len(masks)):
        for f in range(2):
            _, here, there = t_job(m, f)
            got = send(t_ref.at[:, pl.ds(0, TB)], t_dst, ts.at[m, f], tr.at[m, f], me.flip([], True))
            if m + f == 0:
                pl.when(jnp.logical_not(foreign))(here.wait)
                pl.when(foreign)(got.wait_recv)
            else:
                got.wait_recv()
    for m in range(len(masks)):
        for c in range(2):
            to_me, here, there = t_job(m, c)
            if m + c == 0:
                when_not(to_me)(there.wait_send)
            else:
                there.wait_send()
    for u in range(U):
        for m in range(1, len(masks)):
            near(u, m).wait_send()
        across(u).wait()


def split_units(lanes, count):
    tiles = lanes // 128
    units, low = [], 0
    for i in range(count):
        width = tiles // count + (1 if i < tiles % count else 0)
        units.append((low * 128, width * 128))
        low += width
    return units


def gather_inputs(mesh_size, x_t, teacher_t, head_weights, TB):
    R, C = mesh_size
    G = R * C
    nb = log2_of(G)
    masks = G // 2
    lanes = x_t.shape[1]
    units = split_units(lanes, 5)
    U = len(units)
    w_jobs = 2 * (head_weights.shape[1] // HEAD_DIM) * (G // 2 // HEADS)
    return pl.pallas_call(
        functools.partial(gather_kernel, R, C, TB, units),
        out_shape=(
            jax.ShapeDtypeStruct((2,) * nb + (x_t.shape[0], lanes), BF16),
            jax.ShapeDtypeStruct((G, teacher_t.shape[0], TB), BF16),
            jax.ShapeDtypeStruct((3, HEAD_DIM, 128 * R), BF16),
        ),
        in_specs=[pl.BlockSpec(memory_space=pltpu.VMEM)] * 3,
        out_specs=[pl.BlockSpec(memory_space=pltpu.VMEM)] * 3,
        scratch_shapes=[
            DMA((U,)), DMA((U,)), DMA((U, masks)), DMA((U, masks)), DMA((U,)), DMA((U,)), DMA((U,)),
            DMA((masks, 2)), DMA((masks, 2)), DMA(()),
            DMA((w_jobs,)), DMA((R,)), DMA(()),
        ],
        compiler_params=pltpu.CompilerParams(
            collective_id=0, has_side_effects=True, vmem_limit_bytes=VMEM_LIMIT
        ),
    )(x_t, teacher_t, head_weights)


def heads_to_tokens(me, src_at, dst_at, sends, recvs, local):
    jobs = []
    for m in range(1, HEADS):
        other = me.head_xor(m)
        jobs.append(send(src_at(other), dst_at(me.head), sends.at[m], recvs.at[m], me.device_of(other, me.part)))
    return jobs, pltpu.make_async_copy(src_at(me.head), dst_at(me.head), local)


def to_tokens_kernel(R, C, TB, o_ref, a_out, sends, recvs, local):
    me = Place(R, C)
    greet_all(me)
    jobs, here = heads_to_tokens(
        me,
        lambda k: o_ref.at[:, pl.ds(aligned(k, TB), TB)],
        lambda h: a_out.at[pl.ds(aligned(h, HEAD_DIM), HEAD_DIM), :],
        sends, recvs, local,
    )
    for job in jobs:
        job.start()
    here.start()
    here.wait()
    for job in jobs:
        job.wait()


def to_tokens(mesh_size, o_t, TB):
    R, C = mesh_size
    return pl.pallas_call(
        functools.partial(to_tokens_kernel, R, C, TB),
        out_shape=jax.ShapeDtypeStruct((HEADS * HEAD_DIM, TB), BF16),
        in_specs=[pl.BlockSpec(memory_space=pltpu.VMEM)],
        out_specs=pl.BlockSpec(memory_space=pltpu.VMEM),
        scratch_shapes=[DMA((HEADS,)), DMA((HEADS,)), DMA(())],
        compiler_params=pltpu.CompilerParams(
            collective_id=1, has_side_effects=True, vmem_limit_bytes=VMEM_LIMIT
        ),
    )(o_t)


def blocks_to_features(me, src_ref, dst_ref, TB, piece, sends, recvs, local):
    masks = me.masks(me.dims)
    starts, waits = [], []
    dst = dst_ref.at[:, pl.ds(aligned(me.block_of(me.head, me.part), TB), TB)]
    native = me.core == me.tree
    for m, mask in enumerate(masks):
        away = me.flip(mask)
        for f in range(2):
            col = away[2]
            if f:
                col = col + (1 - 2 * me.tree) * me.half
            g = away[1] * me.C + col
            src = src_ref.at[pl.ds(aligned(g, piece), piece), :]
            there = send(src, dst, sends.at[m, f], recvs.at[m, me.core], (me.base + me.tree, away[1], col))
            got = send(src, dst, sends.at[m, f], recvs.at[m, f], me.flip([], True))
            if m + f == 0:
                here = pltpu.make_async_copy(src, dst, local)
                starts += [functools.partial(pl.when(native), here.start)]
                starts += [functools.partial(when_not(native), there.start)]
                waits += [functools.partial(pl.when(native), here.wait)]
                waits += [functools.partial(when_not(native), there.wait_send)]
            else:
                starts.append(there.start)
                waits.append(there.wait_send)
            if m == 0:
                is_local = native & (me.core == f)
                waits.append(functools.partial(when_not(is_local), got.wait_recv))
            else:
                waits.append(got.wait_recv)
    return starts, waits


def to_heads_kernel(R, C, TB, g_ref, y_ref, g_out, y_out, sends, recvs, local, ys, yr, yl):
    me = Place(R, C)
    greet_all(me)
    jobs, here = heads_to_tokens(
        me,
        lambda h: g_ref.at[pl.ds(aligned(h, HEAD_DIM), HEAD_DIM), :],
        lambda k: g_out.at[:, pl.ds(aligned(k, TB), TB)],
        sends, recvs, local,
    )
    for job in jobs:
        job.start()
    here.start()
    starts, waits = blocks_to_features(me, y_ref, y_out, TB, y_out.shape[0], ys, yr, yl)
    for start in starts:
        start()
    here.wait()
    for job in jobs:
        job.wait()
    for wait in waits:
        wait()


def to_heads(mesh_size, g_t, y_t, TB):
    R, C = mesh_size
    blocks = R * C
    features = y_t.shape[0]
    return pl.pallas_call(
        functools.partial(to_heads_kernel, R, C, TB),
        out_shape=(
            jax.ShapeDtypeStruct((HEAD_DIM, HEADS * TB), BF16),
            jax.ShapeDtypeStruct((features // blocks, blocks * TB), BF16),
        ),
        in_specs=[pl.BlockSpec(memory_space=pltpu.VMEM)] * 2,
        out_specs=[pl.BlockSpec(memory_space=pltpu.VMEM)] * 2,
        scratch_shapes=[
            DMA((HEADS,)), DMA((HEADS,)), DMA(()),
            DMA((blocks // 2, 2)), DMA((blocks // 2, 2)), DMA(()),
        ],
        compiler_params=pltpu.CompilerParams(
            collective_id=2, has_side_effects=True, vmem_limit_bytes=VMEM_LIMIT
        ),
    )(g_t, y_t)


def forward_kernel(
    R, C, TB, KC, x_ref, w_ref, b_ref, hot_ref, mask_ref,
    k_out, kt_out, v_out, q_out, o_out, of_out, lse_out, vt_ref,
):
    me = Place(R, C)
    tokens = k_out.shape[0]
    ones_row = (lax.broadcasted_iota(jnp.int32, (16, KC), 0) == 0).astype(F32)
    three_rows = (lax.broadcasted_iota(jnp.int32, (16, KC), 0) < 3).astype(F32)

    def keys(c, _):
        at = pl.ds(aligned(c, KC), KC)
        rows = mm(w_ref[pl.ds(HEAD_DIM, 2 * HEAD_DIM), :], x_ref[:, at]) + b_ref[pl.ds(HEAD_DIM, 2 * HEAD_DIM), :]
        rows = rows.astype(BF16).astype(F32)
        kt, vt = rows[:HEAD_DIM], rows[HEAD_DIM:]
        kt_out[:, at] = kt.astype(BF16)
        vt_ref[pl.ds(0, HEAD_DIM), at] = vt.astype(BF16)
        vt_ref[pl.ds(HEAD_DIM, 16), at] = ones_row.astype(BF16)
        wide = jnp.concatenate([kt, hot_ref[:, at].astype(F32), three_rows, jnp.zeros((32, KC), F32)], axis=0)
        k_out[at, :] = wide.T.astype(BF16)
        wide = jnp.concatenate([vt, three_rows, jnp.zeros((48, KC), F32)], axis=0)
        v_out[at, :] = wide.T.astype(BF16)
        return 0

    lax.fori_loop(0, tokens // KC, keys, 0)

    def block(k, _):
        index = me.block_of(k, me.part)
        at = pl.ds(aligned(index, TB), TB)
        mine = pl.ds(aligned(k, TB), TB)
        rows = mm(w_ref[pl.ds(0, HEAD_DIM), :], x_ref[:, at]) + b_ref[pl.ds(0, HEAD_DIM), :]
        rows = rows.astype(BF16).astype(F32) * HEAD_DIM ** (-0.5)
        wide = jnp.concatenate([rows, mask_ref[:, at].astype(F32), jnp.zeros((48, TB), F32)], axis=0).astype(BF16)
        q_out[:, mine] = wide

        def step(c, carry, diagonal):
            top, total = carry
            span = pl.ds(aligned(c, KC), KC)
            scores = mm(k_out[span, :], wide)
            if diagonal:
                key_pos = c * KC + lax.broadcasted_iota(jnp.int32, (KC, TB), 0)
                query_pos = index * TB + lax.broadcasted_iota(jnp.int32, (KC, TB), 1)
                scores = jnp.where(key_pos <= query_pos, scores, MASKED)
            new_top = jnp.maximum(top, jnp.max(scores, axis=0, keepdims=True))
            weights = jnp.exp(scores - new_top).astype(BF16)
            total = total * jnp.exp(top - new_top) + mm(vt_ref[:, span], weights)
            return new_top, total

        last = (index * TB) // KC
        carry = (jnp.full((1, TB), MASKED, F32), jnp.zeros((HEAD_DIM + 16, TB), F32))
        carry = lax.fori_loop(0, last, lambda c, carry: step(c, carry, False), carry)
        top, total = step(last, carry, True)
        exp_total = total[HEAD_DIM:HEAD_DIM + 1]
        mixed = total[:HEAD_DIM] / exp_total
        o_out[:, mine] = mixed.astype(BF16)
        of_out[:, mine] = mixed
        lse_out[:, mine] = jnp.broadcast_to(top + jnp.log(exp_total), (8, TB))
        return 0

    lax.fori_loop(0, HEADS, block, 0)


def forward_attention(mesh_size, x_all, w, b, hot, mask, TB, KC):
    R, C = mesh_size
    tokens = hot.shape[1]
    mine = HEADS * TB
    spec = pl.BlockSpec(memory_space=pltpu.VMEM)
    return pl.pallas_call(
        functools.partial(forward_kernel, R, C, TB, KC),
        out_shape=(
            jax.ShapeDtypeStruct((tokens, 128), BF16),
            jax.ShapeDtypeStruct((HEAD_DIM, tokens), BF16),
            jax.ShapeDtypeStruct((tokens, 128), BF16),
            jax.ShapeDtypeStruct((128, mine), BF16),
            jax.ShapeDtypeStruct((HEAD_DIM, mine), BF16),
            jax.ShapeDtypeStruct((HEAD_DIM, mine), F32),
            jax.ShapeDtypeStruct((8, mine), F32),
        ),
        in_specs=[spec] * 5,
        out_specs=[spec] * 7,
        scratch_shapes=[pltpu.VMEM((HEAD_DIM + 16, tokens), BF16)],
        compiler_params=pltpu.CompilerParams(vmem_limit_bytes=VMEM_LIMIT),
    )(x_all, w, b, hot, mask)


def three_parts(value):
    high = value.astype(BF16).astype(F32)
    rest = value - high
    middle = rest.astype(BF16).astype(F32)
    return high, middle, rest - middle


def backward_kernel(
    R, C, TB, KC, k_ref, kt_ref, v_ref, q_ref, of_ref, lse_ref, g_ref,
    dq_out, dk_out, dv_out, dk_ref, dv_ref,
):
    me = Place(R, C)
    tokens = k_ref.shape[0]
    dk_ref[...] = jnp.zeros_like(dk_ref)
    dv_ref[...] = jnp.zeros_like(dv_ref)

    def block(k, _):
        index = me.block_of(k, me.part)
        mine = pl.ds(aligned(k, TB), TB)
        grad = g_ref[:, mine]
        delta = jnp.sum(grad.astype(F32) * of_ref[:, mine], axis=0, keepdims=True)
        zeros = jnp.zeros((1, TB), F32)

        def rows(value):
            high, middle, low = three_parts(-value)
            return jnp.concatenate([high, middle, low] + [zeros] * 13, axis=0).astype(BF16)

        query = q_ref[pl.ds(0, HEAD_DIM), mine]
        wide_q = jnp.concatenate(
            [q_ref[pl.ds(0, HEAD_DIM + 16), mine], rows(lse_ref[pl.ds(0, 1), mine]), jnp.zeros((32, TB), BF16)], axis=0
        )
        wide_g = jnp.concatenate([grad, rows(delta), jnp.zeros((48, TB), BF16)], axis=0)

        def step(c, dq, diagonal):
            span = pl.ds(aligned(c, KC), KC)
            probs = jnp.exp(mm(k_ref[span, :], wide_q))
            if diagonal:
                key_pos = c * KC + lax.broadcasted_iota(jnp.int32, (KC, TB), 0)
                query_pos = index * TB + lax.broadcasted_iota(jnp.int32, (KC, TB), 1)
                probs = jnp.where(key_pos <= query_pos, probs, 0.0)
            dscores = (probs * mm(v_ref[span, :], wide_g)).astype(BF16)
            dv_ref[:, span] += mm_nt(grad, probs.astype(BF16))
            dk_ref[:, span] += mm_nt(query, dscores)
            return dq + mm(kt_ref[:, span], dscores)

        last = (index * TB) // KC
        dq = lax.fori_loop(0, last, lambda c, dq: step(c, dq, False), jnp.zeros((HEAD_DIM, TB), F32))
        dq = step(last, dq, True)
        dq_out[:, mine] = (dq * HEAD_DIM ** (-0.5)).astype(BF16)
        return 0

    lax.fori_loop(0, HEADS, block, 0)
    dk_out[...] = dk_ref[...].astype(BF16)
    dv_out[...] = dv_ref[...].astype(BF16)


def backward_attention(mesh_size, k, kt, v, q, of, lse, g, TB, KC):
    R, C = mesh_size
    tokens = k.shape[0]
    spec = pl.BlockSpec(memory_space=pltpu.VMEM)
    return pl.pallas_call(
        functools.partial(backward_kernel, R, C, TB, KC),
        out_shape=(
            jax.ShapeDtypeStruct((HEAD_DIM, HEADS * TB), BF16),
            jax.ShapeDtypeStruct((HEAD_DIM, tokens), BF16),
            jax.ShapeDtypeStruct((HEAD_DIM, tokens), BF16),
        ),
        in_specs=[spec] * 7,
        out_specs=[spec] * 3,
        scratch_shapes=[pltpu.VMEM((HEAD_DIM, tokens), F32)] * 2,
        compiler_params=pltpu.CompilerParams(vmem_limit_bytes=VMEM_LIMIT),
    )(k, kt, v, q, of, lse, g)


def grads_kernel(
    R, C, TB, dq_ref, dk_ref, dv_ref, dw_ref, d_out, kv_out, w_out, part_buf,
    ps, pr, sends, recvs, local, ws, wr, wl,
):
    me = Place(R, C)
    greet_all(me)
    heads_here = (HEADS * HEAD_DIM // C) // HEAD_DIM
    per_head = me.per_head

    w_jobs = []
    for r in range(R):
        to = (me.dp, r, me.head // heads_here)
        to_me = (me.row == r) & (to[2] == me.col)
        slot = me.tree * per_head + lax.rem(me.p, per_head)
        src = dw_ref.at[:, :, pl.ds(r * 128, 128)]
        dst = w_out.at[lax.rem(me.head, heads_here), slot]
        w_jobs.append((
            to_me,
            pltpu.make_async_copy(src, dst, wl),
            send(src, dst, ws.at[r], wr.at[lax.rem(me.head, heads_here), slot], to),
        ))

    p_jobs = []
    for j in range(1, me.S):
        other = lax.rem(me.part + j, me.S)
        for k in range(HEADS):
            src_at = pl.ds(aligned(me.block_of(k, other), TB), TB)
            for i, ref in enumerate((dk_ref, dv_ref)):
                p_jobs.append(send(
                    ref.at[:, src_at], part_buf.at[j - 1, i, :, pl.ds(k * TB, TB)],
                    ps.at[j - 1, i, k], pr.at[j - 1, i, k], me.device_of(me.head, other),
                ))
    for job in p_jobs:
        job.start()
    jobs, here = heads_to_tokens(
        me,
        lambda k: dq_ref.at[:, pl.ds(aligned(k, TB), TB)],
        lambda h: d_out.at[0, pl.ds(aligned(h, HEAD_DIM), HEAD_DIM), :],
        sends.at[0], recvs.at[0], local.at[0],
    )
    heres = [here]
    for job in jobs:
        job.start()
    here.start()
    for job in p_jobs:
        job.wait()
    for i, ref in enumerate((dk_ref, dv_ref)):
        for k in range(HEADS):
            total = ref[:, pl.ds(aligned(me.block_of(k, me.part), TB), TB)].astype(F32)
            for j in range(1, me.S):
                total += part_buf[j - 1, i, :, pl.ds(k * TB, TB)].astype(F32)
            kv_out[i, :, pl.ds(k * TB, TB)] = total.astype(BF16)
    for i in range(2):
        more, here = heads_to_tokens(
            me,
            lambda k: kv_out.at[i, :, pl.ds(aligned(k, TB), TB)],
            lambda h: d_out.at[1 + i, pl.ds(aligned(h, HEAD_DIM), HEAD_DIM), :],
            sends.at[1 + i], recvs.at[1 + i], local.at[1 + i],
        )
        for job in more:
            job.start()
        here.start()
        jobs += more
        heres.append(here)
    for to_me, here, there in w_jobs:
        pl.when(to_me)(here.start)
        when_not(to_me)(there.start)
    for here in heres:
        here.wait()
    for job in jobs:
        job.wait()
    for to_me, here, there in w_jobs:
        pl.when(to_me)(here.wait)
        when_not(to_me)(there.wait_send)
    for i in range(heads_here):
        for t in range(2):
            for j in range(per_head):
                p = (me.col * heads_here + i) * per_head + j
                row, col = p // me.half, t * me.half + lax.rem(p, me.half)
                from_me = (row == me.row) & (col == me.col)
                slot = t * per_head + j
                got = w_out.at[i, slot]
                when_not(from_me)(send(got, got, ws.at[0], wr.at[i, slot], me.flip([], True)).wait_recv)


def grads_home(mesh_size, dq, dk, dv, dw, TB):
    R, C = mesh_size
    per_head = R * C // 2 // HEADS
    S = 2 * per_head
    heads_here = HEADS // C
    return pl.pallas_call(
        functools.partial(grads_kernel, R, C, TB),
        out_shape=(
            jax.ShapeDtypeStruct((3, HEADS * HEAD_DIM, TB), BF16),
            jax.ShapeDtypeStruct((2, HEAD_DIM, HEADS * TB), BF16),
            jax.ShapeDtypeStruct((heads_here, 2 * per_head, 3, HEAD_DIM, 128), BF16),
        ),
        in_specs=[pl.BlockSpec(memory_space=pltpu.VMEM)] * 4,
        out_specs=[pl.BlockSpec(memory_space=pltpu.VMEM)] * 3,
        scratch_shapes=[
            pltpu.VMEM((S - 1, 2, HEAD_DIM, HEADS * TB), BF16),
            DMA((S - 1, 2, HEADS)), DMA((S - 1, 2, HEADS)),
            DMA((3, HEADS)), DMA((3, HEADS)), DMA((3,)),
            DMA((R,)), DMA((heads_here, 2 * per_head)), DMA(()),
        ],
        compiler_params=pltpu.CompilerParams(
            collective_id=3, has_side_effects=True, vmem_limit_bytes=VMEM_LIMIT
        ),
    )(dq, dk, dv, dw)


def features_kernel(R, C, TB, y_ref, y_out, ys, yr, yl):
    me = Place(R, C)
    greet_all(me)
    starts, waits = blocks_to_features(me, y_ref, y_out, TB, y_out.shape[0], ys, yr, yl)
    for start in starts:
        start()
    for wait in waits:
        wait()


def to_features(mesh_size, y_t, TB):
    R, C = mesh_size
    blocks = R * C
    return pl.pallas_call(
        functools.partial(features_kernel, R, C, TB),
        out_shape=jax.ShapeDtypeStruct((y_t.shape[0] // blocks, blocks * TB), y_t.dtype),
        in_specs=[pl.BlockSpec(memory_space=pltpu.VMEM)],
        out_specs=pl.BlockSpec(memory_space=pltpu.VMEM),
        scratch_shapes=[DMA((blocks // 2, 2)), DMA((blocks // 2, 2)), DMA(())],
        compiler_params=pltpu.CompilerParams(
            collective_id=4, has_side_effects=True, vmem_limit_bytes=VMEM_LIMIT
        ),
    )(y_t)


def column_sums(operand):
    return jnp.sum(operand.astype(F32), axis=0)


def shards(
    R, C,
    inputs, memory, teacher, segment_ids, parent_ids, valid_length,
    query_weight, query_bias, key_weight, value_weight, value_bias, proj_weight, proj_bias,
    cross_query_weight, cross_query_bias, cross_key_weight, cross_value_weight, cross_value_bias,
    cross_proj_weight, cross_proj_bias, up_weight, up_bias, down_weight, down_bias,
):
    mesh_size = (R, C)
    me = Place(R, C)
    G = R * C
    tokens = inputs.shape[0]
    mem_rows = memory.shape[0]
    TB = tokens // G
    KC = 512
    w = query_weight.shape[1]
    D = inputs.shape[1] * G
    pairs = lax.axis_size("dp")
    swap = [(i, i ^ 1) for i in range(pairs)]
    native = me.core == me.tree

    ids = jnp.stack([segment_ids, parent_ids])
    ids = jnp.where(native, ids, lax.ppermute(ids, "dp", swap))
    lengths = lax.all_gather(valid_length[0], "dp")
    my_length = lengths[me.base + me.tree]
    count_total = jnp.sum(lengths).astype(F32)
    segment = jnp.arange(16, dtype=jnp.int32)[:, None]
    hot = (ids[0][None] == segment).astype(BF16)
    seen = (segment == ids[0][None]) | (segment == ids[1][None]) | (segment == 0)
    mask = jnp.where(seen, 0.0, MASKED).astype(BF16)

    head_weights = jnp.stack([query_weight.T, key_weight.T, value_weight.T])
    x_t = jnp.concatenate([inputs.T, memory.T], axis=1)
    x_all, teacher_all, w_head = gather_inputs(mesh_size, x_t, teacher.T, head_weights, TB)
    x_all = x_all.reshape(D, tokens + mem_rows)
    teacher_mine = teacher_all.reshape(D, TB).T.astype(F32)
    w_head = w_head.reshape(3 * HEAD_DIM, D)

    across = jnp.concatenate(
        [query_weight, key_weight, value_weight, cross_query_weight, cross_key_weight, cross_value_weight, up_weight],
        axis=1,
    )
    along = jnp.concatenate([proj_weight, cross_proj_weight, down_weight], axis=0)
    across_all = lax.all_gather(across, ("row", "col")).reshape(R, C, across.shape[0], across.shape[1])
    along_all = lax.all_gather(along, ("row", "col")).reshape(R, C, along.shape[0], along.shape[1])

    def across_part(low, width):
        return across_all[:, :, :, low * w:(low + width) * w].transpose(0, 2, 1, 3).reshape(D, width * w * C)

    def along_part(low, width):
        return along_all[:, :, low * w:(low + width) * w].transpose(1, 2, 0, 3).reshape(width * w * C, D)

    Wq, Wk, Wv, Wcq, Wck, Wcv = [across_part(i, 1) for i in range(6)]
    Wup = across_part(6, 4)
    Wproj, Wcproj, Wdown = along_part(0, 1), along_part(1, 1), along_part(2, 4)
    biases = jnp.concatenate([
        query_bias, value_bias, cross_query_bias, cross_value_bias, up_bias, proj_bias, cross_proj_bias, down_bias
    ])
    biases = lax.all_gather(biases, ("row", "col")).astype(F32).reshape(R, C, -1)

    def col_bias(low, width):
        return biases[0, :, low * w:(low + width) * w].reshape(-1)

    def row_bias(index):
        low = 8 * w + index * (D // R)
        return biases[:, 0, low:low + D // R].reshape(-1)

    b_q, b_v, b_cq, b_cv = [col_bias(i, 1) for i in range(4)]
    b_up = col_bias(4, 4)
    b_proj, b_cproj, b_down = [row_bias(i) for i in range(3)]

    def head_slice(vector):
        return lax.dynamic_slice_in_dim(vector, me.head * HEAD_DIM, HEAD_DIM)

    b_head = jnp.concatenate([head_slice(b_q), jnp.zeros((HEAD_DIM,), F32), head_slice(b_v)])[:, None]

    k, kt, v, q, o, of, lse = forward_attention(mesh_size, x_all, w_head, b_head, hot, mask, TB, KC)
    attention = to_tokens(mesh_size, o, TB).T

    block = me.block_of(me.head, me.part)
    x_mine = lax.dynamic_slice_in_dim(x_all, block * TB, TB, axis=1).T
    mem = x_all[:, tokens:].T
    hidden_one = x_mine.astype(F32) + (mm(attention, Wproj) + b_proj)
    hidden_one_b = hidden_one.astype(BF16)
    cross_q = (mm(hidden_one_b, Wcq) + b_cq).astype(BF16)
    cross_k = mm(mem, Wck).astype(BF16)
    cross_v = (mm(mem, Wcv) + b_cv).astype(BF16)

    def heads_of(operand):
        return operand.reshape(operand.shape[0], HEADS, HEAD_DIM)

    scale = HEAD_DIM ** (-0.5)
    scores = jnp.einsum("qhd,khd->hkq", heads_of(cross_q), heads_of(cross_k), preferred_element_type=F32) * scale
    raw = jnp.exp(scores - jnp.max(scores, axis=1, keepdims=True))
    probs = raw / jnp.sum(raw, axis=1, keepdims=True)
    probs_b = probs.astype(BF16)
    cross_out = jnp.einsum(
        "hkq,khd->qhd", probs_b, heads_of(cross_v), preferred_element_type=F32
    ).reshape(TB, D).astype(BF16)
    hidden_two = hidden_one + (mm(cross_out, Wcproj) + b_cproj)
    hidden_two_b = hidden_two.astype(BF16)
    upper = mm(hidden_two_b, Wup) + b_up
    active = jnp.where(upper > 0, upper, 0.0).astype(BF16)
    result = hidden_two + (mm(active, Wdown) + b_down)
    output = result.astype(BF16)
    position = block * TB + jnp.arange(TB, dtype=jnp.int32)
    valid = (position < my_length).astype(F32)[:, None]
    difference = result - teacher_mine
    square_part = jnp.sum(valid * difference * difference)
    grad_result = float(pairs * tokens) / count_total * valid * difference
    grad_out = grad_result.astype(BF16)
    g_down = mm_tn(active, grad_out)
    grad_upper = jnp.where(upper > 0, mm_nt(grad_out, Wdown), 0.0).astype(BF16)
    g_up = mm_tn(hidden_two_b, grad_upper)
    grad_two = grad_result + mm_nt(grad_upper, Wup)
    grad_cross = grad_two.astype(BF16)
    g_cproj = mm_tn(cross_out, grad_cross)
    grad_cross_out = mm_nt(grad_cross, Wcproj).astype(BF16)
    grad_probs = jnp.einsum(
        "qhd,khd->hkq", heads_of(grad_cross_out), heads_of(cross_v), preferred_element_type=F32
    )
    delta = jnp.sum(grad_probs * probs, axis=1, keepdims=True)
    grad_scores = (probs * (grad_probs - delta)).astype(BF16)
    grad_cq = (
        jnp.einsum("hkq,khd->qhd", grad_scores, heads_of(cross_k), preferred_element_type=F32) * scale
    ).reshape(TB, D).astype(BF16)
    grad_ck = (
        jnp.einsum("hkq,qhd->khd", grad_scores, heads_of(cross_q), preferred_element_type=F32) * scale
    ).reshape(mem_rows, D).astype(BF16)
    grad_cv = jnp.einsum(
        "hkq,qhd->khd", probs_b, heads_of(grad_cross_out), preferred_element_type=F32
    ).reshape(mem_rows, D).astype(BF16)
    g_cq = mm_tn(hidden_one_b, grad_cq)
    g_ck = mm_tn(mem, grad_ck)
    g_cv = mm_tn(mem, grad_cv)
    memory_part = (mm_nt(grad_ck, Wck) + mm_nt(grad_cv, Wcv)).astype(BF16)
    grad_one = grad_two + mm_nt(grad_cq, Wcq)
    grad_branch = grad_one.astype(BF16)
    g_proj = mm_tn(attention, grad_branch)
    grad_attention = mm_nt(grad_branch, Wproj).astype(BF16)

    grad_heads, output_t = to_heads(mesh_size, grad_attention.T, output.T, TB)
    dq, dk, dv = backward_attention(mesh_size, k, kt, v, q, of, lse, grad_heads, TB, KC)
    mine = jnp.concatenate([
        lax.dynamic_slice_in_dim(x_all, me.block_of(i, me.part) * TB, TB, axis=1) for i in range(HEADS)
    ], axis=1)
    dw = jnp.stack([mm_nt(dq, mine), mm_nt(dk, x_all[:, :tokens]), mm_nt(dv, x_all[:, :tokens])]).astype(BF16)
    d_tokens, kv_tokens, dw_parts = grads_home(mesh_size, dq, dk, dv, dw, TB)
    bias_q = jnp.sum(dq.astype(F32), axis=1)
    bias_v = jnp.sum(kv_tokens[1].astype(F32), axis=1)
    grad_input = grad_one + mm_tn(d_tokens[0], Wq.T) + mm_tn(d_tokens[1], Wk.T) + mm_tn(d_tokens[2], Wv.T)
    grad_input_t = to_features(mesh_size, grad_input.T.astype(BF16), TB)

    dw_sum = jnp.sum(dw_parts.astype(F32), axis=1)
    dw_sum = dw_sum.transpose(1, 3, 0, 2).reshape(3, D // R, w)

    def across_grad(value):
        return value.astype(BF16).reshape(R, D // R, C, -1).transpose(0, 2, 1, 3).reshape(G, D // R, -1)

    def along_grad(value):
        return value.astype(BF16).reshape(C, -1, R, D // R).transpose(2, 0, 1, 3).reshape(G, -1, D // R)

    across_g = jnp.concatenate([across_grad(g) for g in (g_cq, g_ck, g_cv, g_up)], axis=2)
    along_g = jnp.concatenate([along_grad(g) for g in (g_proj, g_cproj, g_down)], axis=1)
    across_g = lax.psum_scatter(across_g, ("row", "col"), scatter_dimension=0, tiled=True)[0]
    along_g = lax.psum_scatter(along_g, ("row", "col"), scatter_dimension=0, tiled=True)[0]
    memory_sum = lax.psum_scatter(
        jnp.where(me.tree == jnp.arange(2)[:, None, None], memory_part.T[None], 0), "dp", scatter_dimension=0, tiled=True
    ) if pairs == 2 else None
    if pairs != 2:
        both = jnp.where(me.tree == jnp.arange(2)[:, None, None], memory_part.T[None], 0).astype(BF16)
        swapped = lax.ppermute(both, "dp", swap)
        memory_sum = lax.dynamic_slice_in_dim(both + swapped, me.core, 1, axis=0)
    grad_memory = lax.psum_scatter(memory_sum[0], ("row", "col"), scatter_dimension=0, tiled=True)
    place = [jnp.zeros((HEADS, HEAD_DIM), F32).at[me.head].set(b).reshape(-1) for b in (bias_q, bias_v)]
    small = jnp.concatenate(place + [
        column_sums(grad_cq), column_sums(grad_cv), column_sums(grad_upper),
        column_sums(grad_branch), column_sums(grad_cross), column_sums(grad_out), square_part[None],
    ])
    small = lax.psum(small, ("dp", "row", "col"))
    mean_loss = 0.5 * small[-1] / count_total
    low = 0
    vectors = []
    for i, width in enumerate((D, D, D, D, 4 * D, D, D, D)):
        piece = width // (C if i < 5 else R)
        at = low + piece * (me.col if i < 5 else me.row)
        vectors.append(lax.dynamic_slice_in_dim(small, at, piece))
        low += width
    dw_sum, across_g, along_g = [
        lax.psum(g.astype(BF16), "dp").astype(F32) for g in (dw_sum, across_g, along_g)
    ]
    return (
        output_t.T, mean_loss, grad_input_t.T.astype(F32), grad_memory.T.astype(F32),
        dw_sum[0], vectors[0], dw_sum[1], dw_sum[2], vectors[1],
        along_g[:w], vectors[5],
        across_g[:, :w], vectors[2], across_g[:, w:2 * w], across_g[:, 2 * w:3 * w], vectors[3],
        along_g[w:2 * w], vectors[6],
        across_g[:, 3 * w:], vectors[4],
        along_g[2 * w:], vectors[7],
    )


def solution(mesh):
    col, row, both = P("row", "col"), P("col", "row"), P("dp", ("row", "col"))
    in_specs = (
        both, both, both, P("dp"), P("dp"), P("dp"),
        col, P("col"), col, col, P("col"), row, P("row"),
        col, P("col"), col, col, P("col"), row, P("row"),
        col, P("col"), row, P("row"),
    )
    out_specs = (
        both, P(), both, both,
        col, P("col"), col, col, P("col"), row, P("row"),
        col, P("col"), col, col, P("col"), row, P("row"),
        col, P("col"), row, P("row"),
    )
    body = functools.partial(shards, mesh.shape["row"], mesh.shape["col"])
    return jax.shard_map(body, mesh=mesh, in_specs=in_specs, out_specs=out_specs, check_vma=False)
```

time: 1390 us -> 644 us (0.46)
  waiting for transfers between devices: 853 us -> 141 us
  Pallas kernels: 0 us -> 193 us
  matrix products: 191 us -> 72 us
  blocking collectives: 190 us -> 83.3 us
  local copies, waits for them, and re-layouts: 15.9 us -> 96.8 us
  other arithmetic: 111 us -> 30.6 us
    all_gather x12 -> x2, waiting for transfers between devices: 337 us -> 0.02 us  [the longest x1 0.02 us: shards(): lax.all_gather(along, ('row', 'col'))]
    reduce_scatter x13 -> x4, waiting for transfers between devices: 436 us -> 124 us  [the longest x1 85.2 us: shards(): lax.psum_scatter(across_g, ('row', 'col'), scatter_dimension=0, tiled=True)]
    pallas_call x0 -> x7, Pallas kernels: none -> 193 us  [the longest x1 70.8 us: gather_inputs(): pl.pallas_call(functools.partial(gather_kernel, R, C, TB, units), out_sha...]
    psum x2 -> x1, blocking collectives: 173 us -> 37.9 us  [shards(): small = lax.psum(small, ('dp', 'row', 'col'))]
    dot_general x42 -> x32, matrix products: 191 us -> 64.6 us  [the longest x10 18 us: mm_tn(): lax.dot_general(a, b, (((0,), (0,)), ((), ())), preferred_element_type=F32)]
    psum x4 -> x1, waiting for transfers between devices: 78.2 us -> 16.9 us  [shards(): lax.psum(g.astype(BF16), 'dp').astype(F32)]
    convert_element_type x35 -> x8, other arithmetic: 68.7 us -> 13.1 us  [the longest x1 4.58 us: shards(): grad_scores = (probs * (grad_probs - delta)).astype(BF16)]
    unnamed x131 -> x156, local copies, waits for them, and re-layouts: 9.76 us -> 44.9 us
  transfers between devices with their start and end apart: 29 -> 8, of which waited for: 27 -> 3; matrix products, arithmetic and copies ran while one was open for 9% -> 20% of each run, Pallas kernels for 0% -> 30%
where the time goes in v1:
time: 644 us; the launch traced here: 637 us
  Pallas kernels  193 us (30%)
  waiting for transfers between devices  141 us (22%)
  local copies, waits for them, and re-layouts  96.8 us (15%)
  blocking collectives  83.3 us (13%)
  matrix products  72 us (11%)
  other arithmetic  30.6 us (5%)
  between operations  18.6 us (3%)
    reduce_scatter x1, waiting for transfers between devices, shards(): lax.psum_scatter(across_g, ('row', 'col'), scatter_dimension=0, tiled=True)  85.2 us
    pallas_call x1, Pallas kernels, gather_inputs(): pl.pallas_call(functools.partial(gather_kernel, R, C, TB, units), out_sha...  70.8 us
    unnamed x156, local copies, waits for them, and re-layouts  44.9 us
    all_gather x1, blocking collectives, shards(): lax.all_gather(biases, ('row', 'col')).astype(F32).reshape(R, C, -1)  43.6 us
    reduce_scatter x1, waiting for transfers between devices, shards(): lax.psum_scatter(memory_sum[0], ('row', 'col'), scatter_dimension=0, tile...  39 us
    psum x1, blocking collectives, shards(): small = lax.psum(small, ('dp', 'row', 'col'))  37.9 us
    pallas_call x1, Pallas kernels, grads_home(): pl.pallas_call(functools.partial(grads_kernel, R, C, TB), out_shape=(jax....  36.5 us
    pallas_call x1, Pallas kernels, forward_attention(): pl.pallas_call(functools.partial(forward_kernel, R, C, TB, KC), out_shape...  25.6 us
  transfers between devices with their start and end apart: 8, of which 3 were waited for; matrix products, arithmetic and copies ran while one was open for 20% of the time, Pallas kernels for 30%

profile of v1, /device:TPU:0, one launch (start us, length us, event | category | flops | bytes accessed | tf_op | source)
XLA Modules:
  0.0 636.8 jit_solution(18377354411951377810)
XLA Ops:
  31.6 43.6 %all-gather.3 = bf16[16,1,1408]{2,1,0:T(2,128)(2,1)S(1)} all-gather(bf16[1,1,1408]{2,1,0:T(2,128)(2,1)S(1)} %reshape.334), channel_id=3, replica_groups=mesh['dp'=2,'row'=4,'col'=4] {'row','col'}, dimensions={0}, use_global_device_ids=true | all-gather | bytes 47872 | tf_op jit(solution)/shard_map/all_gather | solution.py:762
  80.9 70.8 %shard_map.399 = (bf16[2,2,2,2,32,5120]{5,4,3,2,1,0:T(8,128)(2,1)}, bf16[16,32,256]{2,1,0:T(8,128)(2,1)}, bf16[3,64,512]{2,1,0:T(8,128)(2,1)}) custom-call(bf16[32,5120]{1,0:T(8,128)(2,1)} %pad_maximum_fusion.2.x_ref, bf16[32,4096]{1,0:T(8,128)(2,1)} %bitcast.330, bf16[3,128,128]{2,1,0:T(8,128)(2,1)} %pad_maximum_fusion.5.w_ref), custom_call_target="tpu_custom_call" | custom-call | tf_op jit(solution)/shard_map/pallas_call | solution.py:272
  153.3 25.6 %shard_map.400 = (bf16[4096,128]{1,0:T(8,128)(2,1)}, bf16[64,4096]{1,0:T(8,128)(2,1)}, bf16[4096,128]{1,0:T(8,128)(2,1)}, bf16[128,2048]{1,0:T(8,128)(2,1)}, bf1...) custom-call(bf16[512,5120]{1,0:T(8,128)(2,1)} %bitcast.259, bf16[192,512]{1,0:T(8,128)(2,1)} %bitcast.335, ...), custom_call_target="tpu_custom_call" | custom-call | tf_op jit(solution)/shard_map/pallas_call | solution.py:473
  178.9 11.2 %shard_map.401 = bf16[512,256]{1,0:T(8,128)(2,1)} custom-call(bf16[64,2048]{1,0:T(8,128)(2,1)} %get-tuple-element.66.o_ref), custom_call_target="tpu_custom_call" | custom-call | tf_op jit(solution)/shard_map/pallas_call | solution.py:319
  199.8 3.2 fusion.114
  218.6 7.4 %fusion.121 = (f32[8,256]{1,0:T(8,128)S(1)}, f32[8,1024,256]{2,1,0:T(8,128)}) fusion(bf16[1024,8,64]{0,2,1:T(8,128)(2,1)} %bitcast.320, bf16[256,8,64]{0,2,1:T(8,128)(2,1)} %bitcast.324), kind=kOutput, calls=%fused_computation.199 | convolution fusion | flops 274727936 | bytes 9707520 | tf_op jit(solution)/shard_map/sub | solution.py:797
  226.0 4.8 fusion.29
  240.2 5.1 multiply_reduce_fusion
  245.3 4.9 convert_reduce_fusion.1
  250.2 4.6 multiply_convert_fusion
  260.7 3.1 convolution_convert_fusion.1
  263.8 4.4 reshape.309
  275.5 3.4 convert_reduce_fusion.5
  285.0 3.0 pad_maximum_fusion.1
  299.9 3.1 convolution_convert_fusion.7
  311.2 3.1 pad_maximum_fusion
  332.6 13.4 %shard_map.402 = (bf16[64,2048]{1,0:T(8,128)(2,1)}, bf16[32,4096]{1,0:T(8,128)(2,1)}) custom-call(bf16[512,256]{1,0:T(8,128)(2,1)} %convolution_convert_fusion.8.g_ref, bf16[512,256]{1,0:T(8,128)(2,1)} %get-tuple-element.137.y_ref), custom_call_target="tpu_custom_call" | custom-call | tf_op jit(solution)/shard_map/pallas_call | solution.py:389
  346.0 23.3 %shard_map.403 = (bf16[64,2048]{1,0:T(8,128)(2,1)}, bf16[64,4096]{1,0:T(8,128)(2,1)}, bf16[64,4096]{1,0:T(8,128)(2,1)}) custom-call(bf16[4096,128]{1,0:T(8,128)(2,1)} %get-tuple-element.69.k_ref, bf16[64,4096]{1,0:T(8,128)(2,1)} %get-tuple-element.70.kt_ref, bf16[4096,128]{1,0:T(8,128)(2,1)} %get-tuple-element.71.v_ref, ...), custom_call_target="tpu_custom_call" | custom-call | tf_op jit(solution)/shard_map/pallas_call | solution.py:551
  376.5 36.5 %shard_map.404 = (bf16[3,512,256]{2,1,0:T(8,128)(2,1)}, bf16[2,64,2048]{2,1,0:T(8,128)(2,1)}, bf16[2,2,3,64,128]{4,3,2,1,0:T(8,128)(2,1)}) custom-call(bf16[64,2048]{1,0:T(8,128)(2,1)} %get-tuple-element.76.dq_ref, bf16[64,4096]{1,0:T(8,128)(2,1)} %get-tuple-element.77.dk_ref, bf16[64,4096]{1,0:T(8,128)(2,1)} %get-tuple-element.78.dv_ref, ...), custom_call_target="tpu_custom_call" | custom-call | tf_op jit(solution)/shard_map/pallas_call | solution.py:655
  421.2 12.5 %shard_map.405 = bf16[32,4096]{1,0:T(8,128)(2,1)} custom-call(bf16[512,256]{1,0:T(8,128)(2,1)} %fusion.28.y_ref), custom_call_target="tpu_custom_call" | custom-call | tf_op jit(solution)/shard_map/pallas_call | solution.py:689
  436.3 85.2 %reduce-scatter.11.cloned.1.call-done = bf16[1,128,896]{2,1,0:T(8,128)(2,1)} async-done(((bf16[16,128,896]{2,1,0:T(8,128)(2,1)}), bf16[1,128,896]{2,1,0:T(8,128)(2,1)}) %reduce-scatter.11.cloned.1.call-update) | async-done | bytes 229392 | tf_op jit(solution)/shard_map/reduce_scatter | solution.py:868
  522.2 37.9 %psum.28 = f32[5633]{0:T(1024)S(1)} all-reduce(f32[5633]{0:T(1024)S(1)} %constant_dynamic-update-slice_fusion.10), channel_id=1, replica_groups=mesh['dp'=2,'row'=4,'col'=4] {'dp','row','col'}, use_global_device_ids=true, to_apply=%region_14.15 | all-reduce | flops 5633 | bytes 45064 | tf_op jit(solution)/shard_map/psum | solution.py:883
  562.6 39.0 %reduce-scatter.7.cloned.1.call-done = bf16[32,1024]{1,0:T(8,128)(2,1)} async-done(((bf16[512,1024]{1,0:T(8,128)(2,1)}), bf16[32,1024]{1,0:T(8,128)(2,1)}) %reduce-scatter.7.cloned.1.call-update) | async-done | bytes 65552 | tf_op jit(solution)/shard_map/reduce_scatter | solution.py:877
  603.1 16.9 %all-reduce.4.cloned.1.call-done = (bf16[768,128]{1,0:T(8,128)(2,1)}, bf16[128,896]{1,0:T(8,128)(2,1)}, bf16[3,128,128]{1,2,0:T(8,128)(2,1)}) async-done(((bf16[768,128]{1,0:T(8,128)(2,1)}, bf16[128,896]{1,0:T(8,128)(2,1)}, bf16[3,128,128]{1,2,0:T(8,128)(2,1)}), (bf16[768,128]{1,0:T(8,128)(2,1)}, bf16[128,896]{1,0:T(8,128)(2,1)}, bf16[3,128,128]{1,2,0:T(8,128)(2,1)})) %all-reduce.4.cloned.1.call-update) | async-done | bytes 524304 | tf_op jit(solution)/shard_map/psum | solution.py:893
  (279 shorter events, 152.1 us)
Async XLA Ops:
  7.2 144.6 %copy-start.47 = (s32[4096]{0:T(1024)S(1)}, s32[4096]{0:T(1024)}, u32[]{:S(2)}) copy-start(s32[4096]{0:T(1024)} %param.32) | copy-start | bytes 49156
  7.2 144.6 %copy-start.48 = (s32[4096]{0:T(1024)S(1)}, s32[4096]{0:T(1024)}, u32[]{:S(2)}) copy-start(s32[4096]{0:T(1024)} %param.31) | copy-start | bytes 49156
  7.2 182.9 %all-gather.7.cloned.1.call-start = ((), (), s32[]{:S(2)}) async-start(), calls=%async_computation.8 | async-start | bytes 3342336 | tf_op jit(solution)/shard_map/all_gather | solution.py:748
  8.9 190.9 %all-gather.9.cloned.1.call-start = ((), (), s32[]{:S(2)}) async-start(), calls=%async_computation.9 | async-start | bytes 5570560 | tf_op jit(solution)/shard_map/all_gather | solution.py:747
  15.2 402.7 %reduce-scatter.5.cloned.1.call-start = ((), (), s32[]{:S(2)}) async-start(), calls=%async_computation.4 | async-start | bytes 3145728 | tf_op jit(solution)/shard_map/reduce_scatter | solution.py:870
  18.7 133.1 %collective-permute-start = (s32[2,4096]{1,0:T(2,128)S(1)}, s32[2,4096]{1,0:T(2,128)S(1)}, u32[]{:S(2)}, u32[]{:S(2)}) collective-permute-start(s32[2,4096]{1,0:T(2,128)S(1)} %pad_add_fusion), channel_id=1, source_target_pairs={{0,16},{16,0},{1,17},{17,1},{2,18},{18,2},{3,19},{19,3},{4,20},{20... | collective-permute-start | bytes 98312 | tf_op jit(solution)/shard_map/ppermute | solution.py:726
  259.9 176.5 %reduce-scatter.9.cloned.1.call-start = ((), (), s32[]{:S(2)}) async-start(), calls=%async_computation.6 | async-start | bytes 3342336 | tf_op jit(solution)/shard_map/reduce_scatter | solution.py:869
  288.0 233.5 %reduce-scatter.11.cloned.1.call-start = ((), (), s32[]{:S(2)}) async-start(), calls=%async_computation.7 | async-start | bytes 3899392 | tf_op jit(solution)/shard_map/reduce_scatter | solution.py:868
  314.3 15.0 %copy-start.39 = (bf16[256,512]{0,1:T(8,128)(2,1)S(1)}, bf16[256,512]{0,1:T(8,128)(2,1)}, u32[]{:S(2)}) copy-start(bf16[256,512]{0,1:T(8,128)(2,1)} %copy-done.38) | copy-start | bytes 786436
  314.3 57.4 %slice-start = ((s8[5242880]{0:T(1024)(128)(4,1)}), s8[1048576]{0:T(1024)(128)(4,1)S(1)}, s32[]{:S(2)}) async-start(s8[5242880]{0:T(1024)(128)(4,1)} %bitcast.275), calls=%async_computation.11 | async-start | bytes 2097152
  314.4 15.9 %copy-start.24 = (f32[256,512]{0,1:T(8,128)S(1)}, f32[256,512]{0,1:T(8,128)}, u32[]{:S(2)}) copy-start(f32[256,512]{0,1:T(8,128)} %get-tuple-element.176) | copy-start | bytes 1572868
  314.4 287.2 %reduce-scatter.7.cloned.1.call-start = ((), (), s32[]{:S(2)}) async-start(), calls=%async_computation.5 | async-start | bytes 1114112 | tf_op jit(solution)/shard_map/reduce_scatter | solution.py:877
  330.3 41.5 %slice-start.1 = ((s8[5242880]{0:T(1024)(128)(4,1)}), s8[4194304]{0:T(1024)(128)(4,1)S(1)}, s32[]{:S(2)}) async-start(s8[5242880]{0:T(1024)(128)(4,1)} %bitcast.275), calls=%async_computation.12 | async-start | bytes 8388608
  374.3 38.7 %copy-start.10 = (bf16[64,2048]{1,0:T(8,128)(2,1)S(1)}, bf16[64,2048]{1,0:T(8,128)(2,1)}, u32[]{:S(2)}) copy-start(bf16[64,2048]{1,0:T(8,128)(2,1)} %get-tuple-element.76.dq_ref) | copy-start | bytes 786436
  374.3 41.0 %copy-start.15 = (bf16[4,4,128,128]{3,2,1,0:T(8,128)(2,1)S(1)}, bf16[4,4,128,128]{3,2,1,0:T(8,128)(2,1)}, u32[]{:S(2)}) copy-start(bf16[4,4,128,128]{3,2,1,0:T(8,128)(2,1)} %get-tuple-element.141) | copy-start | bytes 1572868
  374.3 41.4 %copy-start.14 = (bf16[4,4,128,128]{3,2,1,0:T(8,128)(2,1)S(1)}, bf16[4,4,128,128]{3,2,1,0:T(8,128)(2,1)}, u32[]{:S(2)}) copy-start(bf16[4,4,128,128]{3,2,1,0:T(8,128)(2,1)} %get-tuple-element.140) | copy-start | bytes 1572868
  375.7 40.4 %copy-start.13 = (bf16[4,4,128,128]{3,2,1,0:T(8,128)(2,1)S(1)}, bf16[4,4,128,128]{3,2,1,0:T(8,128)(2,1)}, u32[]{:S(2)}) copy-start(bf16[4,4,128,128]{3,2,1,0:T(8,128)(2,1)} %get-tuple-element.139) | copy-start | bytes 1572868
  375.7 40.8 %copy-start.6 = (f32[256,512]{0,1:T(8,128)S(1)}, f32[256,512]{0,1:T(8,128)}, u32[]{:S(2)}) copy-start(f32[256,512]{0,1:T(8,128)} %get-tuple-element.178) | copy-start | bytes 1572868
  375.8 40.8 %copy-start.27 = (f32[256,512]{0,1:T(8,128)S(1)}, f32[256,512]{0,1:T(8,128)}, u32[]{:S(2)}) copy-start(f32[256,512]{0,1:T(8,128)} %get-tuple-element.181) | copy-start | bytes 1572868
  375.8 40.8 %copy-start.28 = (f32[512,256]{1,0:T(8,128)S(1)}, f32[512,256]{1,0:T(8,128)}, u32[]{:S(2)}) copy-start(f32[512,256]{1,0:T(8,128)} %get-tuple-element.138) | copy-start | bytes 1572868
  375.8 40.8 %copy-start.44 = (bf16[16,32,256]{2,1,0:T(8,128)(2,1)S(1)}, bf16[16,32,256]{2,1,0:T(8,128)(2,1)}, u32[]{:S(2)}) copy-start(bf16[16,32,256]{2,1,0:T(8,128)(2,1)} %get-tuple-element.67) | copy-start | bytes 786436
  417.9 15.9 %copy-start.46 = (bf16[2,2,3,64,128]{4,3,2,1,0:T(8,128)(2,1)S(1)}, bf16[2,2,3,64,128]{4,3,2,1,0:T(8,128)(2,1)}, u32[]{:S(2)}) copy-start(bf16[2,2,3,64,128]{4,3,2,1,0:T(8,128)(2,1)} %get-tuple-element.81) | copy-start | bytes 589828
  417.9 202.1 %all-reduce.4.cloned.1.call-start = ((), (), s32[]{:S(2)}) async-start(), calls=%async_computation.10 | async-start | bytes 1048576 | tf_op jit(solution)/shard_map/psum | solution.py:893
  419.2 208.7 %copy-start.45 = (bf16[32,4096]{1,0:T(8,128)(2,1)S(1)}, bf16[32,4096]{1,0:T(8,128)(2,1)}, u32[]{:S(2)}) copy-start(bf16[32,4096]{1,0:T(8,128)(2,1)} %get-tuple-element.68) | copy-start | bytes 786436
  (36 other events, 131.4 us)
Sparse Core Ops, SparseCore 0:
  11.5 70.3 all-gather.6
  84.6 100.5 all-gather.8
  260.0 7.0 reduce-scatter.4
  288.1 140.5 reduce-scatter.8
  431.0 90.4 reduce-scatter.10
  523.7 77.8 reduce-scatter.6
  604.7 15.2 all-reduce.3

commit v2 on v1

--- a/solution.py
+++ b/solution.py
@@ -698,8 +698,186 @@
     )(y_t)
 
 
-def column_sums(operand):
-    return jnp.sum(operand.astype(F32), axis=0)
+def flipped(value):
+    return value.astype(F32).T
+
+
+def token_kernel(
+    R, C, at_ref, x_ref, teacher_ref, across_ref, along_ref, rows_ref, up_row_ref, valid_ref, factor_ref, mine_ref,
+    ga_out, y_out, one_out, across_out, along_out, mem_out, rows_out, up_row_out,
+    wcq, wck, wcv, wup, wproj, wcproj, wdown, ck, cv, ckt, cvt, probs_ref, ot_ref, q_ref, g_ref, dqt_ref, dck, dcv,
+):
+    TB = at_ref.shape[1]
+    D = at_ref.shape[0]
+    rows_r = D // R
+    w = D // C
+    mem_rows = ck.shape[0]
+    tokens = x_ref.shape[1] - mem_rows
+    scale = HEAD_DIM ** (-0.5)
+
+    def gather_across(dst, low, width):
+        for r in range(R):
+            dst[pl.ds(r * rows_r, rows_r), :] = jnp.concatenate(
+                [across_ref[r * C + c, :, pl.ds(low * w, width * w)] for c in range(C)], axis=1
+            )
+
+    def gather_along(dst, low, width):
+        for c in range(C):
+            dst[pl.ds(c * width * w, width * w), :] = jnp.concatenate(
+                [along_ref[r * C + c, pl.ds(low * w, width * w), :] for r in range(R)], axis=1
+            )
+
+    gather_along(wproj, 0, 1)
+    gather_across(wcq, 3, 1)
+    gather_across(wck, 4, 1)
+    gather_across(wcv, 5, 1)
+    gather_along(wcproj, 1, 1)
+    gather_across(wup, 6, 4)
+    gather_along(wdown, 2, 4)
+
+    b_cq, b_cv, b_proj, b_cproj, b_down = [rows_ref[pl.ds(i, 1), :] for i in range(5)]
+
+    mem_t = x_ref[:, pl.ds(tokens, mem_rows)]
+    mem = flipped(mem_t).astype(BF16)
+    ck[...] = mm(mem, wck[...]).astype(BF16)
+    cv[...] = (mm(mem, wcv[...]) + b_cv).astype(BF16)
+    ckt[...] = flipped(ck[...]).astype(BF16)
+    cvt[...] = flipped(cv[...]).astype(BF16)
+
+    attention = flipped(at_ref[...]).astype(BF16)
+    x_mine = flipped(mine_ref[...])
+    hidden_one = x_mine + (mm(attention, wproj[...]) + b_proj)
+    hidden_one_b = hidden_one.astype(BF16)
+    q_ref[...] = (mm(hidden_one_b, wcq[...]) + b_cq).astype(BF16)
+
+    lane = lax.broadcasted_iota(jnp.int32, (TB, 128), 1)
+
+    def halves(value):
+        zero = jnp.zeros_like(value)
+        return [jnp.where((lane < HEAD_DIM) if i == 0 else (lane >= HEAD_DIM), value, zero) for i in range(2)]
+
+    def cross_forward(pair, _):
+        at = pl.ds(aligned(pair, 128), 128)
+        query = halves((q_ref[:, at].astype(F32) * scale).astype(BF16))
+        for i in range(2):
+            scores = mm_nt(ck[:, at], query[i])
+            raw = jnp.exp(scores - jnp.max(scores, axis=0, keepdims=True))
+            probs = (raw * (1.0 / jnp.sum(raw, axis=0, keepdims=True))).astype(BF16)
+            probs_ref[pair * 2 + i] = probs
+            head = pl.ds(aligned(pair * 2 + i, HEAD_DIM), HEAD_DIM)
+            ot_ref[head, :] = mm(cvt[head, :], probs)
+        return 0
+
+    lax.fori_loop(0, HEADS // 2, cross_forward, 0)
+    cross_out = ot_ref[...].T.astype(BF16)
+    hidden_two = hidden_one + (mm(cross_out, wcproj[...]) + b_cproj)
+    hidden_two_b = hidden_two.astype(BF16)
+    active = jnp.maximum(mm(hidden_two_b, wup[...]) + up_row_ref[...], 0.0).astype(BF16)
+    result = hidden_two + (mm(active, wdown[...]) + b_down)
+    y_out[...] = result.T.astype(BF16)
+    difference = (result - flipped(teacher_ref[...])) * valid_ref[...]
+    rows_out[pl.ds(5, 1), :] = jnp.sum(difference * difference, axis=0, keepdims=True)
+    grad_result = factor_ref[...] * difference
+    grad_out = grad_result.astype(BF16)
+
+    def sums(value):
+        return jnp.sum(value.astype(F32), axis=0, keepdims=True)
+
+    def put_along(low, width, left, right):
+        for c in range(C):
+            part = mm_tn(left[:, c * width * w:(c + 1) * width * w], right).astype(BF16)
+            for r in range(R):
+                along_out[r * C + c, pl.ds(low * w, width * w), :] = part[:, r * rows_r:(r + 1) * rows_r]
+
+    def put_across(low, width, left, right):
+        for r in range(R):
+            part = mm_tn(left[:, r * rows_r:(r + 1) * rows_r], right).astype(BF16)
+            for c in range(C):
+                across_out[r * C + c, :, pl.ds(low * w, width * w)] = part[:, c * width * w:(c + 1) * width * w]
+
+    rows_out[pl.ds(4, 1), :] = sums(grad_out)
+    put_along(2, 4, active, grad_out)
+    grad_active = mm_nt(grad_out, wdown[...])
+    grad_upper = jnp.where(active > 0, grad_active, 0.0).astype(BF16)
+    up_row_out[...] = sums(grad_upper)
+    put_across(3, 4, hidden_two_b, grad_upper)
+    grad_two = grad_result + mm_nt(grad_upper, wup[...])
+    grad_cross = grad_two.astype(BF16)
+    rows_out[pl.ds(3, 1), :] = sums(grad_cross)
+    put_along(1, 1, cross_out, grad_cross)
+    grad_cross_out = mm_nt(grad_cross, wcproj[...]).astype(BF16)
+    g_ref[...] = grad_cross_out
+    ot_ref[...] = ot_ref[...] * flipped(grad_cross_out)
+
+    def cross_backward(pair, _):
+        at = pl.ds(aligned(pair, 128), 128)
+        query = halves((q_ref[:, at].astype(F32) * scale).astype(BF16))
+        grad = halves(g_ref[:, at])
+        dk = jnp.zeros((mem_rows, 128), F32)
+        dv = jnp.zeros((mem_rows, 128), F32)
+        for i in range(2):
+            head = pl.ds(aligned(pair * 2 + i, HEAD_DIM), HEAD_DIM)
+            delta = jnp.sum(ot_ref[head, :], axis=0, keepdims=True)
+            probs = probs_ref[pair * 2 + i]
+            dprobs = mm_nt(cv[:, at], grad[i])
+            dscores = (probs.astype(F32) * (dprobs - delta)).astype(BF16)
+            dqt_ref[head, :] = mm(ckt[head, :], dscores) * scale
+            dk += mm(dscores, query[i])
+            dv += mm(probs, grad[i])
+        dck[:, at] = dk.astype(BF16)
+        dcv[:, at] = dv.astype(BF16)
+        return 0
+
+    lax.fori_loop(0, HEADS // 2, cross_backward, 0)
+    grad_cq = dqt_ref[...].T.astype(BF16)
+    rows_out[pl.ds(0, 1), :] = sums(grad_cq)
+    rows_out[pl.ds(1, 1), :] = sums(dcv[...])
+    put_across(0, 1, hidden_one_b, grad_cq)
+    put_across(1, 1, mem, dck[...])
+    put_across(2, 1, mem, dcv[...])
+    mem_out[...] = (mm_nt(wck[...], dck[...]) + mm_nt(wcv[...], dcv[...])).astype(BF16)
+    grad_one = grad_two + mm_nt(grad_cq, wcq[...])
+    one_out[...] = grad_one
+    grad_branch = grad_one.astype(BF16)
+    rows_out[pl.ds(2, 1), :] = sums(grad_branch)
+    put_along(0, 1, attention, grad_branch)
+    ga_out[...] = mm_nt(wproj[...], grad_branch).astype(BF16)
+
+
+def token_block(mesh_size, at, x_all, teacher, across_all, along_all, rows, up_row, valid, factor, x_mine):
+    R, C = mesh_size
+    D, TB = at.shape
+    G = R * C
+    w = D // C
+    tokens = TB * G
+    mem_rows = x_all.shape[1] - tokens
+    FF = 4 * D
+    spec = pl.BlockSpec(memory_space=pltpu.VMEM)
+    return pl.pallas_call(
+        functools.partial(token_kernel, R, C),
+        out_shape=(
+            jax.ShapeDtypeStruct((D, TB), BF16),
+            jax.ShapeDtypeStruct((D, TB), BF16),
+            jax.ShapeDtypeStruct((TB, D), F32),
+            jax.ShapeDtypeStruct((G, D // R, 7 * w), BF16),
+            jax.ShapeDtypeStruct((G, 6 * w, D // R), BF16),
+            jax.ShapeDtypeStruct((D, mem_rows), BF16),
+            jax.ShapeDtypeStruct((8, D), F32),
+            jax.ShapeDtypeStruct((1, FF), F32),
+        ),
+        in_specs=[spec] * 10,
+        out_specs=[spec] * 8,
+        scratch_shapes=[
+            pltpu.VMEM((D, D), BF16), pltpu.VMEM((D, D), BF16), pltpu.VMEM((D, D), BF16), pltpu.VMEM((D, FF), BF16),
+            pltpu.VMEM((D, D), BF16), pltpu.VMEM((D, D), BF16), pltpu.VMEM((FF, D), BF16),
+            pltpu.VMEM((mem_rows, D), BF16), pltpu.VMEM((mem_rows, D), BF16),
+            pltpu.VMEM((D, mem_rows), BF16), pltpu.VMEM((D, mem_rows), BF16),
+            pltpu.VMEM((HEADS, mem_rows, TB), BF16),
+            pltpu.VMEM((D, TB), F32), pltpu.VMEM((TB, D), BF16), pltpu.VMEM((TB, D), BF16), pltpu.VMEM((D, TB), F32),
+            pltpu.VMEM((mem_rows, D), BF16), pltpu.VMEM((mem_rows, D), BF16),
+        ],
+        compiler_params=pltpu.CompilerParams(vmem_limit_bytes=VMEM_LIMIT),
+    )(at, x_all, teacher, across_all, along_all, rows, up_row, valid, factor, x_mine)
 
 
 def shards(
@@ -736,7 +914,6 @@
     x_t = jnp.concatenate([inputs.T, memory.T], axis=1)
     x_all, teacher_all, w_head = gather_inputs(mesh_size, x_t, teacher.T, head_weights, TB)
     x_all = x_all.reshape(D, tokens + mem_rows)
-    teacher_mine = teacher_all.reshape(D, TB).T.astype(F32)
     w_head = w_head.reshape(3 * HEAD_DIM, D)
 
     across = jnp.concatenate(
@@ -750,12 +927,7 @@
     def across_part(low, width):
         return across_all[:, :, :, low * w:(low + width) * w].transpose(0, 2, 1, 3).reshape(D, width * w * C)
 
-    def along_part(low, width):
-        return along_all[:, :, low * w:(low + width) * w].transpose(1, 2, 0, 3).reshape(width * w * C, D)
-
-    Wq, Wk, Wv, Wcq, Wck, Wcv = [across_part(i, 1) for i in range(6)]
-    Wup = across_part(6, 4)
-    Wproj, Wcproj, Wdown = along_part(0, 1), along_part(1, 1), along_part(2, 4)
+    Wq, Wk, Wv = [across_part(i, 1) for i in range(3)]
     biases = jnp.concatenate([
         query_bias, value_bias, cross_query_bias, cross_value_bias, up_bias, proj_bias, cross_proj_bias, down_bias
     ])
@@ -778,71 +950,20 @@
     b_head = jnp.concatenate([head_slice(b_q), jnp.zeros((HEAD_DIM,), F32), head_slice(b_v)])[:, None]
 
     k, kt, v, q, o, of, lse = forward_attention(mesh_size, x_all, w_head, b_head, hot, mask, TB, KC)
-    attention = to_tokens(mesh_size, o, TB).T
+    attention_t = to_tokens(mesh_size, o, TB)
 
     block = me.block_of(me.head, me.part)
-    x_mine = lax.dynamic_slice_in_dim(x_all, block * TB, TB, axis=1).T
-    mem = x_all[:, tokens:].T
-    hidden_one = x_mine.astype(F32) + (mm(attention, Wproj) + b_proj)
-    hidden_one_b = hidden_one.astype(BF16)
-    cross_q = (mm(hidden_one_b, Wcq) + b_cq).astype(BF16)
-    cross_k = mm(mem, Wck).astype(BF16)
-    cross_v = (mm(mem, Wcv) + b_cv).astype(BF16)
-
-    def heads_of(operand):
-        return operand.reshape(operand.shape[0], HEADS, HEAD_DIM)
-
-    scale = HEAD_DIM ** (-0.5)
-    scores = jnp.einsum("qhd,khd->hkq", heads_of(cross_q), heads_of(cross_k), preferred_element_type=F32) * scale
-    raw = jnp.exp(scores - jnp.max(scores, axis=1, keepdims=True))
-    probs = raw / jnp.sum(raw, axis=1, keepdims=True)
-    probs_b = probs.astype(BF16)
-    cross_out = jnp.einsum(
-        "hkq,khd->qhd", probs_b, heads_of(cross_v), preferred_element_type=F32
-    ).reshape(TB, D).astype(BF16)
-    hidden_two = hidden_one + (mm(cross_out, Wcproj) + b_cproj)
-    hidden_two_b = hidden_two.astype(BF16)
-    upper = mm(hidden_two_b, Wup) + b_up
-    active = jnp.where(upper > 0, upper, 0.0).astype(BF16)
-    result = hidden_two + (mm(active, Wdown) + b_down)
-    output = result.astype(BF16)
+    x_mine = lax.dynamic_slice_in_dim(x_all, block * TB, TB, axis=1)
     position = block * TB + jnp.arange(TB, dtype=jnp.int32)
     valid = (position < my_length).astype(F32)[:, None]
-    difference = result - teacher_mine
-    square_part = jnp.sum(valid * difference * difference)
-    grad_result = float(pairs * tokens) / count_total * valid * difference
-    grad_out = grad_result.astype(BF16)
-    g_down = mm_tn(active, grad_out)
-    grad_upper = jnp.where(upper > 0, mm_nt(grad_out, Wdown), 0.0).astype(BF16)
-    g_up = mm_tn(hidden_two_b, grad_upper)
-    grad_two = grad_result + mm_nt(grad_upper, Wup)
-    grad_cross = grad_two.astype(BF16)
-    g_cproj = mm_tn(cross_out, grad_cross)
-    grad_cross_out = mm_nt(grad_cross, Wcproj).astype(BF16)
-    grad_probs = jnp.einsum(
-        "qhd,khd->hkq", heads_of(grad_cross_out), heads_of(cross_v), preferred_element_type=F32
+    factor = (float(pairs * tokens) / count_total).reshape(1, 1)
+    rows = jnp.stack([b_cq, b_cv, b_proj, b_cproj, b_down] + [jnp.zeros((D,), F32)] * 3)
+    grad_attention_t, output_mine, grad_one, across_g, along_g, memory_part, row_sums, up_sums = token_block(
+        mesh_size, attention_t, x_all, teacher_all.reshape(D, TB), across_all.reshape(G, D // R, -1),
+        along_all.reshape(G, -1, D // R), rows, b_up[None], valid, factor, x_mine,
     )
-    delta = jnp.sum(grad_probs * probs, axis=1, keepdims=True)
-    grad_scores = (probs * (grad_probs - delta)).astype(BF16)
-    grad_cq = (
-        jnp.einsum("hkq,khd->qhd", grad_scores, heads_of(cross_k), preferred_element_type=F32) * scale
-    ).reshape(TB, D).astype(BF16)
-    grad_ck = (
-        jnp.einsum("hkq,qhd->khd", grad_scores, heads_of(cross_q), preferred_element_type=F32) * scale
-    ).reshape(mem_rows, D).astype(BF16)
-    grad_cv = jnp.einsum(
-        "hkq,qhd->khd", probs_b, heads_of(grad_cross_out), preferred_element_type=F32
-    ).reshape(mem_rows, D).astype(BF16)
-    g_cq = mm_tn(hidden_one_b, grad_cq)
-    g_ck = mm_tn(mem, grad_ck)
-    g_cv = mm_tn(mem, grad_cv)
-    memory_part = (mm_nt(grad_ck, Wck) + mm_nt(grad_cv, Wcv)).astype(BF16)
-    grad_one = grad_two + mm_nt(grad_cq, Wcq)
-    grad_branch = grad_one.astype(BF16)
-    g_proj = mm_tn(attention, grad_branch)
-    grad_attention = mm_nt(grad_branch, Wproj).astype(BF16)
-
-    grad_heads, output_t = to_heads(mesh_size, grad_attention.T, output.T, TB)
+
+    grad_heads, output_t = to_heads(mesh_size, grad_attention_t, output_mine, TB)
     dq, dk, dv = backward_attention(mesh_size, k, kt, v, q, of, lse, grad_heads, TB, KC)
     mine = jnp.concatenate([
         lax.dynamic_slice_in_dim(x_all, me.block_of(i, me.part) * TB, TB, axis=1) for i in range(HEADS)
@@ -857,28 +978,19 @@
     dw_sum = jnp.sum(dw_parts.astype(F32), axis=1)
     dw_sum = dw_sum.transpose(1, 3, 0, 2).reshape(3, D // R, w)
 
-    def across_grad(value):
-        return value.astype(BF16).reshape(R, D // R, C, -1).transpose(0, 2, 1, 3).reshape(G, D // R, -1)
-
-    def along_grad(value):
-        return value.astype(BF16).reshape(C, -1, R, D // R).transpose(2, 0, 1, 3).reshape(G, -1, D // R)
-
-    across_g = jnp.concatenate([across_grad(g) for g in (g_cq, g_ck, g_cv, g_up)], axis=2)
-    along_g = jnp.concatenate([along_grad(g) for g in (g_proj, g_cproj, g_down)], axis=1)
     across_g = lax.psum_scatter(across_g, ("row", "col"), scatter_dimension=0, tiled=True)[0]
     along_g = lax.psum_scatter(along_g, ("row", "col"), scatter_dimension=0, tiled=True)[0]
     memory_sum = lax.psum_scatter(
-        jnp.where(me.tree == jnp.arange(2)[:, None, None], memory_part.T[None], 0), "dp", scatter_dimension=0, tiled=True
+        jnp.where(me.tree == jnp.arange(2)[:, None, None], memory_part[None], 0), "dp", scatter_dimension=0, tiled=True
     ) if pairs == 2 else None
     if pairs != 2:
-        both = jnp.where(me.tree == jnp.arange(2)[:, None, None], memory_part.T[None], 0).astype(BF16)
+        both = jnp.where(me.tree == jnp.arange(2)[:, None, None], memory_part[None], 0).astype(BF16)
         swapped = lax.ppermute(both, "dp", swap)
         memory_sum = lax.dynamic_slice_in_dim(both + swapped, me.core, 1, axis=0)
     grad_memory = lax.psum_scatter(memory_sum[0], ("row", "col"), scatter_dimension=0, tiled=True)
     place = [jnp.zeros((HEADS, HEAD_DIM), F32).at[me.head].set(b).reshape(-1) for b in (bias_q, bias_v)]
     small = jnp.concatenate(place + [
-        column_sums(grad_cq), column_sums(grad_cv), column_sums(grad_upper),
-        column_sums(grad_branch), column_sums(grad_cross), column_sums(grad_out), square_part[None],
+        row_sums[0], row_sums[1], up_sums[0], row_sums[2], row_sums[3], row_sums[4], jnp.sum(row_sums[5])[None],
     ])
     small = lax.psum(small, ("dp", "row", "col"))
     mean_loss = 0.5 * small[-1] / count_total

time: 644 us -> 596 us (0.925)
  matrix products: 72 us -> 8.53 us
  waiting for transfers between devices: 141 us -> 203 us
  local copies, waits for them, and re-layouts: 96.8 us -> 43.3 us
  Pallas kernels: 193 us -> 220 us
  other arithmetic: 30.6 us -> 17.5 us
    reduce_scatter x1, waiting for transfers between devices: 0.01 us -> 52.9 us  [shards(): lax.psum_scatter(along_g, ('row', 'col'), scatter_dimension=0, tiled=True)]
    dot_general x12 -> x0, matrix products: 34 us -> none  [the longest x7 14.5 us: mm(): return jnp.dot(a, b, preferred_element_type=F32)]
    pallas_call x0 -> x1, Pallas kernels: none -> 31 us  [token_block(): pl.pallas_call(functools.partial(token_kernel, R, C), out_shape=(jax.Shap...]
    unnamed x156 -> x80, local copies, waits for them, and re-layouts: 44.9 us -> 27.6 us
    dot_general x10 -> x3, matrix products: 18 us -> 1.6 us  [mm_tn(): lax.dot_general(a, b, (((0,), (0,)), ((), ())), preferred_element_type=F32)]
    reshape x7 -> x0, local copies, waits for them, and re-layouts: 16.1 us -> none  [the longest x3 8.44 us: along_grad(): value.astype(BF16).reshape(C, -1, R, D // R).transpose(2, 0, 1, 3)]
    transpose x7 -> x0, local copies, waits for them, and re-layouts: 12.5 us -> none  [the longest x4 7.3 us: across_grad(): value.astype(BF16).reshape(R, D // R, C, -1).transpose(0, 2, 1, 3)]
    reduce_scatter x1, waiting for transfers between devices: 85.2 us -> 92.8 us  [shards(): lax.psum_scatter(across_g, ('row', 'col'), scatter_dimension=0, tiled=True)]
  transfers between devices with their start and end apart: 8 -> 8, of which waited for: 3 -> 4; matrix products, arithmetic and copies ran while one was open for 20% -> 9% of each run, Pallas kernels for 30% -> 32%
where the time goes in v2:
time: 596 us; the launch traced here: 594 us
  Pallas kernels  220 us (37%)
  waiting for transfers between devices  203 us (34%)
  blocking collectives  82.7 us (14%)
  local copies, waits for them, and re-layouts  43.3 us (7%)
  between operations  18 us (3%)
  other arithmetic  17.5 us (3%)
  matrix products  8.53 us (1%)
    reduce_scatter x1, waiting for transfers between devices, shards(): lax.psum_scatter(across_g, ('row', 'col'), scatter_dimension=0, tiled=True)  92.8 us
    pallas_call x1, Pallas kernels, gather_inputs(): pl.pallas_call(functools.partial(gather_kernel, R, C, TB, units), out_sha...  67.8 us
    reduce_scatter x1, waiting for transfers between devices, shards(): lax.psum_scatter(along_g, ('row', 'col'), scatter_dimension=0, tiled=True)  52.9 us
    all_gather x1, blocking collectives, shards(): lax.all_gather(biases, ('row', 'col')).astype(F32).reshape(R, C, -1)  43.4 us
    reduce_scatter x1, waiting for transfers between devices, shards(): lax.psum_scatter(memory_sum[0], ('row', 'col'), scatter_dimension=0, tile...  39 us
    psum x1, blocking collectives, shards(): small = lax.psum(small, ('dp', 'row', 'col'))  37.5 us
    pallas_call x1, Pallas kernels, grads_home(): pl.pallas_call(functools.partial(grads_kernel, R, C, TB), out_shape=(jax....  33.1 us
    pallas_call x1, Pallas kernels, token_block(): pl.pallas_call(functools.partial(token_kernel, R, C), out_shape=(jax.Shap...  31 us
  transfers between devices with their start and end apart: 8, of which 4 were waited for; matrix products, arithmetic and copies ran while one was open for 9% of the time, Pallas kernels for 32%

profile of v2, /device:TPU:0, one launch (start us, length us, event | category | flops | bytes accessed | tf_op | source)
XLA Modules:
  0.0 593.9 jit_solution(6521080781297785378)
XLA Ops:
  7.3 1.6 pad_maximum_fusion.1
  19.2 1.8 all-reduce
  30.5 43.4 %all-gather.3 = bf16[16,1,1408]{2,1,0:T(2,128)(2,1)S(1)} all-gather(bf16[1,1,1408]{2,1,0:T(2,128)(2,1)S(1)} %reshape.206), channel_id=2, replica_groups=mesh['dp'=2,'row'=4,'col'=4] {'row','col'}, dimensions={0}, use_global_device_ids=true | all-gather | bytes 47872 | tf_op jit(solution)/shard_map/all_gather | solution.py:934
  76.3 67.8 %shard_map.399 = (bf16[2,2,2,2,32,5120]{5,4,3,2,1,0:T(8,128)(2,1)}, bf16[16,32,256]{2,1,0:T(8,128)(2,1)}, bf16[3,64,512]{2,1,0:T(8,128)(2,1)}) custom-call(bf16[32,5120]{1,0:T(8,128)(2,1)} %pad_maximum_fusion.x_ref, bf16[32,4096]{1,0:T(8,128)(2,1)} %bitcast.134, bf16[3,128,128]{2,1,0:T(8,128)(2,1)} %pad_maximum_fusion.3.w_ref), custom_call_target="tpu_custom_call" | custom-call | tf_op jit(solution)/shard_map/pallas_call | solution.py:272
  152.6 1.8 dynamic-slice_dynamic-update-slice_fusion
  159.3 25.6 %shard_map.400 = (bf16[4096,128]{1,0:T(8,128)(2,1)}, bf16[64,4096]{1,0:T(8,128)(2,1)}, bf16[4096,128]{1,0:T(8,128)(2,1)}, bf16[128,2048]{1,0:T(8,128)(2,1)}, bf1...) custom-call(bf16[512,5120]{1,0:T(8,128)(2,1)} %bitcast.117, bf16[192,512]{1,0:T(8,128)(2,1)} %bitcast.137, ...), custom_call_target="tpu_custom_call" | custom-call | tf_op jit(solution)/shard_map/pallas_call | solution.py:473
  184.9 13.8 %shard_map.401.at_ref = bf16[512,256]{1,0:T(8,128)(2,1)} custom-call(bf16[64,2048]{1,0:T(8,128)(2,1)} %get-tuple-element.74.o_ref), custom_call_target="tpu_custom_call" | custom-call | tf_op jit(solution)/shard_map/pallas_call | solution.py:319
  198.8 31.0 %shard_map.402 = (bf16[512,256]{1,0:T(8,128)(2,1)}, bf16[512,256]{1,0:T(8,128)(2,1)}, f32[256,512]{1,0:T(8,128)}, bf16[16,128,896]{2,1,0:T(8,128)(2,1)}, bf16[16...) custom-call(bf16[512,256]{1,0:T(8,128)(2,1)} %shard_map.401.at_ref, ...), custom_call_target="tpu_custom_call" | custom-call | tf_op jit(solution)/shard_map/pallas_call | solution.py:856
  229.9 2.8 broadcast_select_fusion
  234.7 12.8 %shard_map.403 = (bf16[64,2048]{1,0:T(8,128)(2,1)}, bf16[32,4096]{1,0:T(8,128)(2,1)}) custom-call(bf16[512,256]{1,0:T(8,128)(2,1)} %get-tuple-element.76.g_ref, bf16[512,256]{1,0:T(8,128)(2,1)} %get-tuple-element.77.y_ref), custom_call_target="tpu_custom_call" | custom-call | tf_op jit(solution)/shard_map/pallas_call | solution.py:389
  247.4 23.2 %shard_map.404 = (bf16[64,2048]{1,0:T(8,128)(2,1)}, bf16[64,4096]{1,0:T(8,128)(2,1)}, bf16[64,4096]{1,0:T(8,128)(2,1)}) custom-call(bf16[4096,128]{1,0:T(8,128)(2,1)} %get-tuple-element.79.k_ref, bf16[64,4096]{1,0:T(8,128)(2,1)} %get-tuple-element.80.kt_ref, bf16[4096,128]{1,0:T(8,128)(2,1)} %get-tuple-element.81.v_ref, ...), custom_call_target="tpu_custom_call" | custom-call | tf_op jit(solution)/shard_map/pallas_call | solution.py:551
  270.6 1.9 fusion.18
  272.5 3.7 fusion.15
  278.3 33.1 %shard_map.405 = (bf16[3,512,256]{2,1,0:T(8,128)(2,1)}, bf16[2,64,2048]{2,1,0:T(8,128)(2,1)}, bf16[2,2,3,64,128]{4,3,2,1,0:T(8,128)(2,1)}) custom-call(bf16[64,2048]{1,0:T(8,128)(2,1)} %get-tuple-element.86.dq_ref, bf16[64,4096]{1,0:T(8,128)(2,1)} %get-tuple-element.87.dk_ref, bf16[64,4096]{1,0:T(8,128)(2,1)} %get-tuple-element.88.dv_ref, ...), custom_call_target="tpu_custom_call" | custom-call | tf_op jit(solution)/shard_map/pallas_call | solution.py:655
  311.6 1.6 fusion.37
  317.2 12.9 %shard_map.406 = bf16[32,4096]{1,0:T(8,128)(2,1)} custom-call(bf16[512,256]{1,0:T(8,128)(2,1)} %fusion.5.y_ref), custom_call_target="tpu_custom_call" | custom-call | tf_op jit(solution)/shard_map/pallas_call | solution.py:689
  331.7 1.8 convert_bitcast_fusion
  333.5 52.9 %reduce-scatter.9.cloned.1.call-done = bf16[1,768,128]{2,1,0:T(8,128)(2,1)} async-done(((bf16[16,768,128]{2,1,0:T(8,128)(2,1)}), bf16[1,768,128]{2,1,0:T(8,128)(2,1)}) %reduce-scatter.9.cloned.1.call-update) | async-done | bytes 196624 | tf_op jit(solution)/shard_map/reduce_scatter | solution.py:982
  386.4 92.8 %reduce-scatter.11.cloned.1.call-done = bf16[1,128,896]{2,1,0:T(8,128)(2,1)} async-done(((bf16[16,128,896]{2,1,0:T(8,128)(2,1)}), bf16[1,128,896]{2,1,0:T(8,128)(2,1)}) %reduce-scatter.11.cloned.1.call-update) | async-done | bytes 229392 | tf_op jit(solution)/shard_map/reduce_scatter | solution.py:981
  479.9 37.5 %psum.28 = f32[5633]{0:T(1024)S(1)} all-reduce(f32[5633]{0:T(1024)S(1)} %constant_dynamic-update-slice_fusion.10), channel_id=1, replica_groups=mesh['dp'=2,'row'=4,'col'=4] {'dp','row','col'}, use_global_device_ids=true, to_apply=%region_5.6 | all-reduce | flops 5633 | bytes 45064 | tf_op jit(solution)/shard_map/psum | solution.py:995
  519.9 39.0 %reduce-scatter.7.cloned.1.call-done = bf16[32,1024]{1,0:T(8,128)(2,1)} async-done(((bf16[512,1024]{1,0:T(8,128)(2,1)}), bf16[32,1024]{1,0:T(8,128)(2,1)}) %reduce-scatter.7.cloned.1.call-update) | async-done | bytes 65552 | tf_op jit(solution)/shard_map/reduce_scatter | solution.py:990
  560.4 16.9 %all-reduce.4.cloned.1.call-done = (bf16[768,128]{1,0:T(8,128)(2,1)}, bf16[128,896]{1,0:T(8,128)(2,1)}, bf16[3,128,128]{1,2,0:T(8,128)(2,1)}) async-done(((bf16[768,128]{1,0:T(8,128)(2,1)}, bf16[128,896]{1,0:T(8,128)(2,1)}, bf16[3,128,128]{1,2,0:T(8,128)(2,1)}), (bf16[768,128]{1,0:T(8,128)(2,1)}, bf16[128,896]{1,0:T(8,128)(2,1)}, bf16[3,128,128]{1,2,0:T(8,128)(2,1)})) %all-reduce.4.cloned.1.call-update) | async-done | bytes 524304 | tf_op jit(solution)/shard_map/psum | solution.py:1005
  577.3 1.6 slice.193
  580.5 1.6 slice.194
  (155 shorter events, 52.9 us)
Async XLA Ops:
  7.2 68.3 %copy-start.6 = (bf16[4096,32]{0,1:T(8,128)(2,1)S(1)}, bf16[4096,32]{0,1:T(8,128)(2,1)}, u32[]{:S(2)}) copy-start(bf16[4096,32]{0,1:T(8,128)(2,1)} %param.28) | copy-start | bytes 786436
  7.2 68.3 %copy-start.10 = (bf16[1024,32]{0,1:T(8,128)(2,1)S(1)}, bf16[1024,32]{0,1:T(8,128)(2,1)}, u32[]{:S(2)}) copy-start(bf16[1024,32]{0,1:T(8,128)(2,1)} %param.29) | copy-start | bytes 196612
  7.2 191.6 %all-gather.9.cloned.1.call-start = ((), (), s32[]{:S(2)}) async-start(), calls=%async_computation.9 | async-start | bytes 3342336 | tf_op jit(solution)/shard_map/all_gather | solution.py:925
  8.9 189.9 %all-gather.7.cloned.1.call-start = ((), (), s32[]{:S(2)}) async-start(), calls=%async_computation.8 | async-start | bytes 5570560 | tf_op jit(solution)/shard_map/all_gather | solution.py:924
  15.2 301.1 %reduce-scatter.5.cloned.1.call-start = ((), (), s32[]{:S(2)}) async-start(), calls=%async_computation.4 | async-start | bytes 3145728 | tf_op jit(solution)/shard_map/reduce_scatter | solution.py:983
  18.7 139.1 %collective-permute-start = (s32[2,4096]{1,0:T(2,128)S(1)}, s32[2,4096]{1,0:T(2,128)S(1)}, u32[]{:S(2)}, u32[]{:S(2)}) collective-permute-start(s32[2,4096]{1,0:T(2,128)S(1)} %pad_add_fusion), channel_id=1, source_target_pairs={{0,16},{16,0},{1,17},{17,1},{2,18},{18,2},{3,19},{19,3},{4,20},{20... | collective-permute-start | bytes 98312 | tf_op jit(solution)/shard_map/ppermute | solution.py:904
  146.5 11.3 %copy-start.11 = (s32[4096]{0:T(1024)S(1)}, s32[4096]{0:T(1024)}, u32[]{:S(2)}) copy-start(s32[4096]{0:T(1024)} %param.32) | copy-start | bytes 49156
  146.5 11.2 %copy-start.12 = (s32[4096]{0:T(1024)S(1)}, s32[4096]{0:T(1024)}, u32[]{:S(2)}) copy-start(s32[4096]{0:T(1024)} %param.31) | copy-start | bytes 49156
  232.7 153.7 %reduce-scatter.9.cloned.1.call-start = ((), (), s32[]{:S(2)}) async-start(), calls=%async_computation.6 | async-start | bytes 3342336 | tf_op jit(solution)/shard_map/reduce_scatter | solution.py:982
  233.3 245.9 %reduce-scatter.11.cloned.1.call-start = ((), (), s32[]{:S(2)}) async-start(), calls=%async_computation.7 | async-start | bytes 3899392 | tf_op jit(solution)/shard_map/reduce_scatter | solution.py:981
  233.9 325.1 %reduce-scatter.7.cloned.1.call-start = ((), (), s32[]{:S(2)}) async-start(), calls=%async_computation.5 | async-start | bytes 1114112 | tf_op jit(solution)/shard_map/reduce_scatter | solution.py:990
  247.4 28.7 %slice-start = ((s8[5242880]{0:T(1024)(128)(4,1)}), s8[1048576]{0:T(1024)(128)(4,1)S(1)}, s32[]{:S(2)}) async-start(s8[5242880]{0:T(1024)(128)(4,1)} %bitcast.120), calls=%async_computation.11 | async-start | bytes 2097152
  270.6 1.9 copy-start.2
  270.6 5.6 slice-start.1
  272.5 3.7 copy-start.3
  277.6 33.8 %copy-start.4 = (f32[256,512]{1,0:T(8,128)S(1)}, f32[256,512]{1,0:T(8,128)}, u32[]{:S(2)}) copy-start(f32[256,512]{1,0:T(8,128)} %get-tuple-element.92) | copy-start | bytes 1572868
  313.2 1.3 copy-start.9
  313.2 1.4 copy-start.1
  314.9 1.4 copy-start
  314.9 1.6 copy-start.8
  315.3 15.8 %copy-start.13 = (f32[8,512]{1,0:T(8,128)S(1)}, f32[8,512]{1,0:T(8,128)}, u32[]{:S(2)}) copy-start(f32[8,512]{1,0:T(8,128)} %get-tuple-element.90) | copy-start | bytes 49156
  315.3 16.4 %copy-start.14 = (f32[1,2048]{1,0:T(1,128)S(1)}, f32[1,2048]{1,0:T(1,128)}, u32[]{:S(2)}) copy-start(f32[1,2048]{1,0:T(1,128)} %get-tuple-element.91) | copy-start | bytes 24580
  316.3 261.0 %all-reduce.4.cloned.1.call-start = ((), (), s32[]{:S(2)}) async-start(), calls=%async_computation.10 | async-start | bytes 1048576 | tf_op jit(solution)/shard_map/psum | solution.py:1005
  331.7 253.5 %copy-start.7 = (bf16[32,4096]{1,0:T(8,128)(2,1)S(1)}, bf16[32,4096]{1,0:T(8,128)(2,1)}, u32[]{:S(2)}) copy-start(bf16[32,4096]{1,0:T(8,128)(2,1)} %get-tuple-element.78) | copy-start | bytes 786436
  (2 other events, 1.4 us)
Sparse Core Ops, SparseCore 0:
  11.5 71.0 all-gather.8
  85.3 95.8 all-gather.6
  232.8 7.3 reduce-scatter.4
  245.9 140.5 reduce-scatter.8
  388.7 90.4 reduce-scatter.10
  481.4 77.5 reduce-scatter.6
  562.0 15.2 all-reduce.3
